TPU v7x, 512 devices: a whole 4x8x8 slice. The times are simulated.
512 devices in a mesh: section: 16 (over x, z_lo), tp: 4 (over z_hi, core), dp: 8 (over y).
Axes of the slice: x: 4, y: 8, z: 8 (z_hi: 2, z_lo: 4; z = z_hi * 4 + z_lo), core: 2. Of those that a mesh axis runs over, the one named last changes fastest.
Arguments:
- inputs: bfloat16 [4, 384, 7168], P(None, 'dp', 'tp'), may hold values from -6 to 6
- norm_gain: float32 [16, 7168], P('section', 'tp'), may hold values from 0.25 to 1.75
- norm_bias: float32 [16, 7168], P('section', 'tp'), may hold values from -3 to 3
- mix: bfloat16 [16, 56, 128, 128], P('section', 'tp'), may hold values from -0.5 to 0.5
Outputs:
- gain_grad: float32 [16, 7168], P('section', 'tp')
- bias_grad: float32 [16, 7168], P('section', 'tp')
- mix_grad: float32 [16, 56, 128, 128], P('section', 'tp', 'dp')
All inputs are finite; a program needn't handle non-finite values.
Results may differ from a plain program's by a relative error of at most 0.0011.
Values may be sent and summed in bfloat16 or wider, within the bound.
A program may use at most 64 MiB of HBM per device.

v0:
```python
import math

import jax
import jax.numpy as jnp
from jax import lax
from jax.sharding import PartitionSpec as P

EPSILON = 1e-05
GRAD_EPS = 1e-06
GELU_K = math.sqrt(2.0 / math.pi)
GELU_C = 0.044715


def swapped(x, axis, apart):
    return lax.ppermute(x, axis, [(i, i ^ 1 << apart) for i in range(lax.axis_size(axis))])


def from_behind(block, axis, distance):
    devices = range(lax.axis_size(axis))
    route = [(i - distance, i) for i in devices if i - distance in devices]
    return lax.ppermute(block, axis, route)


def gelu_tanh(value):
    return 0.5 * value * (1.0 + jnp.tanh(GELU_K * (value + GELU_C * value * value * value)))


def gelu_slope(value):
    tangent = jnp.tanh(GELU_K * (value + GELU_C * value * value * value))
    return 0.5 * (1.0 + tangent) + 0.5 * value * (1.0 - tangent * tangent) * GELU_K * (
        1.0 + 3.0 * GELU_C * value * value
    )


def head_norm(wide_in, head_count, head_size):
    row_count = wide_in.shape[0]
    split_in = wide_in.reshape(row_count, head_count, head_size)
    mean_val = jnp.mean(split_in, axis=-1, keepdims=True)
    centred = split_in - mean_val
    variance = jnp.mean(centred * centred, axis=-1, keepdims=True)
    inv_std = lax.rsqrt(variance + EPSILON)
    return (centred * inv_std, inv_std)


def keep_slot(buffer, value, position, active):
    previous = lax.dynamic_index_in_dim(buffer, position, 0, False)
    return lax.dynamic_update_index_in_dim(buffer, jnp.where(active, value, previous), position, 0)


def mirror(payload, section_count):
    for bit_index in range(section_count.bit_length() - 1):
        payload = swapped(payload, "section", bit_index)
    return payload


def shards(inputs, norm_gain, norm_bias, mix):
    section_count = lax.axis_size("section")
    section_index = lax.axis_index("section")
    batches, row_count, feature_count = inputs.shape
    head_count, head_size = (mix.shape[1], mix.shape[2])
    feature_total = feature_count * lax.axis_size("tp")
    param_count = section_count * (
        2 * feature_total + head_count * lax.axis_size("tp") * head_size * head_size
    )
    gain_row = norm_gain[0]
    bias_row = norm_bias[0]
    weights = mix[0]
    loss_scale = 1.0 / math.sqrt(batches * row_count * lax.axis_size("dp"))
    is_first = section_index == 0
    is_last = section_index == section_count - 1
    tick_count = batches + 2 * section_count - 1

    def one_tick(tick_now, state_now):
        fwd_in, bwd_in, last_out, kept_blocks, saved_act, saved_grad, grad_gain, grad_bias = (
            state_now
        )
        fwd_batch = tick_now - section_index
        fwd_on = (fwd_batch >= 0) & (fwd_batch < batches)
        fwd_pos = jnp.clip(fwd_batch, 0, batches - 1)
        back_batch = tick_now - (2 * section_count - 1 - section_index)
        back_on = (back_batch >= 0) & (back_batch < batches)
        back_pos = jnp.clip(back_batch, 0, batches - 1)
        entering = jnp.where(is_first, lax.dynamic_index_in_dim(inputs, fwd_pos, 0, False), fwd_in)
        stored = lax.dynamic_index_in_dim(kept_blocks, back_pos, 0, False)
        top_grad = (last_out.astype(jnp.float32) * loss_scale).astype(jnp.bfloat16)
        grad_out = jnp.where(is_last, top_grad, bwd_in)
        fwd_wide = entering.astype(jnp.float32)
        bwd_wide = stored.astype(jnp.float32)
        normed_fwd, inv_fwd = head_norm(fwd_wide, head_count, head_size)
        normed_bwd3, inv_bwd = head_norm(bwd_wide, head_count, head_size)
        normed_fwd = normed_fwd.reshape(row_count, feature_count)
        normed_bwd = normed_bwd3.reshape(row_count, feature_count)
        act_fwd = gelu_tanh(normed_fwd * gain_row + bias_row).astype(jnp.bfloat16)
        mixed_out = jnp.einsum(
            "rhk,hkj->rhj",
            act_fwd.reshape(row_count, head_count, head_size),
            weights,
            preferred_element_type=jnp.float32,
        )
        output = (fwd_wide + mixed_out.reshape(row_count, feature_count)).astype(jnp.bfloat16)
        pre_bwd = normed_bwd * gain_row + bias_row
        act_bwd = gelu_tanh(pre_bwd).astype(jnp.bfloat16)
        grad_act = jnp.einsum(
            "rhj,hkj->rhk",
            grad_out.reshape(row_count, head_count, head_size),
            weights,
            preferred_element_type=jnp.float32,
        )
        grad_pre = grad_act.reshape(row_count, feature_count) * gelu_slope(pre_bwd)
        grad_norm = (grad_pre * gain_row).reshape(row_count, head_count, head_size)
        grad_centred = inv_bwd * (
            grad_norm
            - jnp.mean(grad_norm, axis=-1, keepdims=True)
            - normed_bwd3 * jnp.mean(grad_norm * normed_bwd3, axis=-1, keepdims=True)
        )
        grad_in = (
            grad_out.astype(jnp.float32) + grad_centred.reshape(row_count, feature_count)
        ).astype(jnp.bfloat16)
        grad_gain = grad_gain + jnp.where(back_on, jnp.sum(grad_pre * normed_bwd, axis=0), 0.0)
        grad_bias = grad_bias + jnp.where(back_on, jnp.sum(grad_pre, axis=0), 0.0)
        kept_blocks = keep_slot(kept_blocks, entering, fwd_pos, fwd_on)
        saved_act = keep_slot(saved_act, act_bwd, back_pos, back_on)
        saved_grad = keep_slot(saved_grad, grad_out, back_pos, back_on)
        fwd_next = from_behind(output, "section", 1)
        bwd_next = from_behind(grad_in, "section", -1)
        return (
            fwd_next,
            bwd_next,
            output,
            kept_blocks,
            saved_act,
            saved_grad,
            grad_gain,
            grad_bias,
        )

    blocks_zero = jnp.zeros((batches, row_count, feature_count), jnp.bfloat16)
    rows_zero = jnp.zeros((row_count, feature_count), jnp.bfloat16)
    vector_zero = jnp.zeros((feature_count,), jnp.float32)
    state_now = (
        rows_zero,
        rows_zero,
        rows_zero,
        blocks_zero,
        blocks_zero,
        blocks_zero,
        vector_zero,
        vector_zero,
    )
    lend_most = max(0, (min(batches, 2 * section_count - 1) - 1) // 2)
    is_lower = section_index < section_count // 2
    own_live = jnp.minimum(batches, 2 * (section_count - section_index) - 1)
    mirror_live = jnp.minimum(batches, 2 * section_index + 1)
    lend_count = jnp.where(is_lower, jnp.maximum(0, (own_live - mirror_live) // 2), 0)
    lent_mask = (jnp.arange(lend_most) < lend_count)[:, None, None]
    slots_zero = jnp.zeros((lend_most, row_count, feature_count), jnp.bfloat16)
    first_stop = section_count // 2 - 1 + lend_most
    second_stop = 3 * section_count // 2
    state_now = lax.fori_loop(0, first_stop, one_tick, state_now)
    head_slots = state_now[3][:lend_most]
    held_blocks = mirror(jnp.where(lent_mask, head_slots, slots_zero), section_count)
    kept_blocks = state_now[3].at[:lend_most].set(jnp.where(lent_mask, slots_zero, head_slots))
    state_now = state_now[:3] + (kept_blocks,) + state_now[4:]
    state_now = lax.fori_loop(first_stop, second_stop, one_tick, state_now)
    returned = mirror(jnp.where(is_lower, slots_zero, held_blocks), section_count)
    kept_blocks = (
        state_now[3].at[:lend_most].set(jnp.where(lent_mask, returned, state_now[3][:lend_most]))
    )
    state_now = state_now[:3] + (kept_blocks,) + state_now[4:]
    state_now = lax.fori_loop(second_stop, tick_count, one_tick, state_now)
    saved_act, saved_grad, grad_gain, grad_bias = (
        state_now[4],
        state_now[5],
        state_now[6],
        state_now[7],
    )
    mix_local = jnp.einsum(
        "mrhk,mrhj->hkj",
        saved_act.reshape(batches, row_count, head_count, head_size),
        saved_grad.reshape(batches, row_count, head_count, head_size),
        preferred_element_type=jnp.float32,
    )
    mix_share = lax.psum_scatter(mix_local, "dp", scatter_dimension=1, tiled=True)
    gain_total, bias_total = lax.psum((grad_gain, grad_bias), "dp")
    local_squares = jnp.sum(mix_share * mix_share) + (
        jnp.sum(gain_total * gain_total) + jnp.sum(bias_total * bias_total)
    ) / lax.axis_size("dp")
    total = lax.psum(local_squares, ("section", "tp", "dp"))
    scale = lax.rsqrt(total / param_count + GRAD_EPS)
    return ((gain_total * scale)[None], (bias_total * scale)[None], (mix_share * scale)[None])


def solution(mesh):
    placed = (
        P(None, "dp", "tp"),
        P("section", "tp"),
        P("section", "tp"),
        P("section", "tp", None, None),
    )
    return jax.shard_map(
        shards,
        mesh=mesh,
        in_specs=placed,
        out_specs=(P("section", "tp"), P("section", "tp"), P("section", "tp", "dp", None)),
        check_vma=False,
    )
```

profile of v0, /device:TPU:1, one launch (start us, length us, event | category | flops | bytes accessed | tf_op | source)
XLA Modules:
  0.0 906.1 jit_solution(3942942154675389595)
XLA Ops:
  9.3 135.1 %while.89 = (s32[]{:T(128)}, bf16[48,1792]{1,0:T(8,128)(2,1)S(1)}, bf16[48,1792]{1,0:T(8,128)(2,1)S(1)}, bf16[48,1792]{1,0:T(8,128)(2,1)S(1)}, bf16[4,48,1792]{2...) while((s32[]{:T(128)}, bf16[48,1792]{1,0:T(8,128)(2,1)S(1)}, ...), condition=%wide.region_9.10_spmd.clone, body=%wide.region_0.9_spmd.clone.sunk | while | flops 51618124 | bytes 17632748 | solution.py:159
  81.5 7.4 collective-permute-start.4
  99.5 7.2 collective-permute-start.4
  117.2 7.1 collective-permute-start.4
  153.7 12.8 %collective-permute-start.7 = (bf16[1,48,1792]{2,1,0:T(8,128)(2,1)S(1)}, bf16[1,48,1792]{2,1,0:T(8,128)(2,1)S(1)}, u32[]{:S(2)}, u32[]{:S(2)}) collective-permute-start(bf16[1,48,1792]{2,1,0:T(8,128)(2,1)S(1)} %collective-permute-done.6), channel_id=1, source_target_pairs={{0,64},{32,96},{64,0},{96,32},{128,192},{160,224},{192,128},{224,1... | collective-permute-start | bytes 516104 | tf_op jit(solution)/shard_map/ppermute | solution.py:15
  215.9 277.8 %while.87 = (s32[]{:T(128)}, bf16[48,1792]{1,0:T(8,128)(2,1)S(1)}, bf16[48,1792]{1,0:T(8,128)(2,1)S(1)}, bf16[48,1792]{1,0:T(8,128)(2,1)S(1)}, bf16[4,48,1792]{2...) while((s32[]{:T(128)}, bf16[48,1792]{1,0:T(8,128)(2,1)S(1)}, ...), condition=%wide.region_19.20_spmd, body=%wide.region_10.19_spmd.sunk | while | flops 51528528 | bytes 19467784 | solution.py:164
  283.7 7.5 collective-permute-start
  319.4 7.6 collective-permute-start
  337.6 7.2 collective-permute-start
  355.3 7.2 collective-permute-start
  373.1 7.1 collective-permute-start
  390.8 7.1 collective-permute-start
  408.5 7.6 collective-permute-start
  426.6 8.3 collective-permute-start
  445.4 8.3 collective-permute-start
  464.2 8.3 collective-permute-start
  483.1 8.3 collective-permute-start
  494.7 206.4 %while.88 = (s32[]{:T(128)}, bf16[48,1792]{1,0:T(8,128)(2,1)S(1)}, bf16[48,1792]{1,0:T(8,128)(2,1)S(1)}, bf16[48,1792]{1,0:T(8,128)(2,1)S(1)}, bf16[4,48,1792]{2...) while((s32[]{:T(128)}, bf16[48,1792]{1,0:T(8,128)(2,1)S(1)}, ...), condition=%wide.region_29.30_spmd, body=%wide.region_20.29_spmd.sunk | while | flops 51528528 | bytes 19467784 | solution.py:170
  503.0 7.4 collective-permute-start.2
  520.9 8.3 collective-permute-start.2
  539.7 8.3 collective-permute-start.2
  558.6 8.2 collective-permute-start.2
  577.3 8.4 collective-permute-start.2
  596.3 8.3 collective-permute-start.2
  615.1 8.3 collective-permute-start.2
  633.9 8.3 collective-permute-start.2
  652.8 8.3 collective-permute-start.2
  671.6 8.3 collective-permute-start.2
  690.5 8.3 collective-permute-start.2
  703.6 22.4 %all-reduce = (f32[1792]{0:T(1024)S(1)}, f32[1792]{0:T(1024)S(1)}) all-reduce(f32[1792]{0:T(1024)S(1)} %get-tuple-element.1044, f32[1792]{0:T(1024)S(1)} %get-tuple-element.1047), channel_id=1, replica_groups=mesh['section'=16,'tp'=4,'dp'=8] {'dp'}, use_global_device_ids=true, to_apply=%region_30.31 | all-reduce | flops 3584 | bytes 28672 | tf_op jit(solution)/shard_map/psum | solution.py:184
  728.0 64.0 %reduce-scatter.2.cloned.1.call-done = f32[14,16,128]{2,1,0:T(8,128)} async-done(((f32[14,128,128]{2,1,0:T(8,128)}), f32[14,16,128]{2,1,0:T(8,128)}) %reduce-scatter.2.cloned.1.call-update) | async-done | bytes 114704 | tf_op jit(solution)/shard_map/reduce_scatter | solution.py:183
  794.3 102.4 %psum.23 = f32[]{:T(128)} all-reduce(f32[]{:T(128)S(6)} %add.771), channel_id=1, replica_groups=mesh['section'=16,'tp'=4,'dp'=8] {'section','tp','dp'}, use_global_device_ids=true, to_apply=%region_36.37 | all-reduce | flops 1 | bytes 8 | tf_op jit(solution)/shard_map/psum | solution.py:188
  (1508 shorter events, 483.2 us)
Async XLA Ops:
  7.2 784.8 %reduce-scatter.2.cloned.1.call-start = ((), (), s32[]{:S(2)}) async-start(), calls=%async_computation.1 | async-start | bytes 1032192 | tf_op jit(solution)/shard_map/reduce_scatter | solution.py:183
  11.3 11.7 %collective-permute-start.5 = (bf16[48,1792]{1,0:T(8,128)(2,1)S(1)}, bf16[48,1792]{1,0:T(8,128)(2,1)S(1)}, u32[]{:S(2)}, u32[]{:S(2)}) collective-permute-start(bf16[48,1792]{1,0:T(8,128)(2,1)S(1)} %fusion.143), channel_id=1, source_target_pairs={{32,0},{64,32},{96,64},{128,96},{160,128},{192,160},{224,192},{256... | collective-permute-start | bytes 516104 | tf_op jit(solution)/shard_map/while/body/eval_jaxpr/ppermute | solution.py:21
  58.4 12.6 %collective-permute-start.5 = (bf16[48,1792]{1,0:T(8,128)(2,1)S(1)}, bf16[48,1792]{1,0:T(8,128)(2,1)S(1)}, u32[]{:S(2)}, u32[]{:S(2)}) collective-permute-start(bf16[48,1792]{1,0:T(8,128)(2,1)S(1)} %fusion.143), channel_id=1, source_target_pairs={{32,0},{64,32},{96,64},{128,96},{160,128},{192,160},{224,192},{256... | collective-permute-start | bytes 516104 | tf_op jit(solution)/shard_map/while/body/eval_jaxpr/ppermute | solution.py:21
  75.3 13.7 %collective-permute-start.5 = (bf16[48,1792]{1,0:T(8,128)(2,1)S(1)}, bf16[48,1792]{1,0:T(8,128)(2,1)S(1)}, u32[]{:S(2)}, u32[]{:S(2)}) collective-permute-start(bf16[48,1792]{1,0:T(8,128)(2,1)S(1)} %fusion.143), channel_id=1, source_target_pairs={{32,0},{64,32},{96,64},{128,96},{160,128},{192,160},{224,192},{256... | collective-permute-start | bytes 516104 | tf_op jit(solution)/shard_map/while/body/eval_jaxpr/ppermute | solution.py:21
  93.3 13.4 %collective-permute-start.5 = (bf16[48,1792]{1,0:T(8,128)(2,1)S(1)}, bf16[48,1792]{1,0:T(8,128)(2,1)S(1)}, u32[]{:S(2)}, u32[]{:S(2)}) collective-permute-start(bf16[48,1792]{1,0:T(8,128)(2,1)S(1)} %fusion.143), channel_id=1, source_target_pairs={{32,0},{64,32},{96,64},{128,96},{160,128},{192,160},{224,192},{256... | collective-permute-start | bytes 516104 | tf_op jit(solution)/shard_map/while/body/eval_jaxpr/ppermute | solution.py:21
  111.0 13.4 %collective-permute-start.5 = (bf16[48,1792]{1,0:T(8,128)(2,1)S(1)}, bf16[48,1792]{1,0:T(8,128)(2,1)S(1)}, u32[]{:S(2)}, u32[]{:S(2)}) collective-permute-start(bf16[48,1792]{1,0:T(8,128)(2,1)S(1)} %fusion.143), channel_id=1, source_target_pairs={{32,0},{64,32},{96,64},{128,96},{160,128},{192,160},{224,192},{256... | collective-permute-start | bytes 516104 | tf_op jit(solution)/shard_map/while/body/eval_jaxpr/ppermute | solution.py:21
  128.7 13.4 %collective-permute-start.5 = (bf16[48,1792]{1,0:T(8,128)(2,1)S(1)}, bf16[48,1792]{1,0:T(8,128)(2,1)S(1)}, u32[]{:S(2)}, u32[]{:S(2)}) collective-permute-start(bf16[48,1792]{1,0:T(8,128)(2,1)S(1)} %fusion.143), channel_id=1, source_target_pairs={{32,0},{64,32},{96,64},{128,96},{160,128},{192,160},{224,192},{256... | collective-permute-start | bytes 516104 | tf_op jit(solution)/shard_map/while/body/eval_jaxpr/ppermute | solution.py:21
  153.7 19.3 %collective-permute-start.7 = (bf16[1,48,1792]{2,1,0:T(8,128)(2,1)S(1)}, bf16[1,48,1792]{2,1,0:T(8,128)(2,1)S(1)}, u32[]{:S(2)}, u32[]{:S(2)}) collective-permute-start(bf16[1,48,1792]{2,1,0:T(8,128)(2,1)S(1)} %collective-permute-done.6), channel_id=1, source_target_pairs={{0,64},{32,96},{64,0},{96,32},{128,192},{160,224},{192,128},{224,1... | collective-permute-start | bytes 516104 | tf_op jit(solution)/shard_map/ppermute | solution.py:15
  210.7 283.0 %collective-permute-start.13 = (bf16[1,48,1792]{2,1,0:T(8,128)(2,1)}, bf16[1,48,1792]{2,1,0:T(8,128)(2,1)}, u32[]{:S(2)}, u32[]{:S(2)}) collective-permute-start(bf16[1,48,1792]{2,1,0:T(8,128)(2,1)} %collective-permute-done.12), channel_id=1, source_target_pairs={{0,256},{32,288},{64,320},{96,352},{128,384},{160,416},{192,448},{... | collective-permute-start | bytes 516104 | tf_op jit(solution)/shard_map/ppermute | solution.py:15
  277.5 13.7 %collective-permute-start.1 = (bf16[48,1792]{1,0:T(8,128)(2,1)S(1)}, bf16[48,1792]{1,0:T(8,128)(2,1)S(1)}, u32[]{:S(2)}, u32[]{:S(2)}) collective-permute-start(bf16[48,1792]{1,0:T(8,128)(2,1)S(1)} %fusion.129), channel_id=1, source_target_pairs={{32,0},{64,32},{96,64},{128,96},{160,128},{192,160},{224,192},{256... | collective-permute-start | bytes 516104 | tf_op jit(solution)/shard_map/while/body/eval_jaxpr/ppermute | solution.py:21
  295.6 13.3 %collective-permute-start.1 = (bf16[48,1792]{1,0:T(8,128)(2,1)S(1)}, bf16[48,1792]{1,0:T(8,128)(2,1)S(1)}, u32[]{:S(2)}, u32[]{:S(2)}) collective-permute-start(bf16[48,1792]{1,0:T(8,128)(2,1)S(1)} %fusion.129), channel_id=1, source_target_pairs={{32,0},{64,32},{96,64},{128,96},{160,128},{192,160},{224,192},{256... | collective-permute-start | bytes 516104 | tf_op jit(solution)/shard_map/while/body/eval_jaxpr/ppermute | solution.py:21
  313.2 13.9 %collective-permute-start.1 = (bf16[48,1792]{1,0:T(8,128)(2,1)S(1)}, bf16[48,1792]{1,0:T(8,128)(2,1)S(1)}, u32[]{:S(2)}, u32[]{:S(2)}) collective-permute-start(bf16[48,1792]{1,0:T(8,128)(2,1)S(1)} %fusion.129), channel_id=1, source_target_pairs={{32,0},{64,32},{96,64},{128,96},{160,128},{192,160},{224,192},{256... | collective-permute-start | bytes 516104 | tf_op jit(solution)/shard_map/while/body/eval_jaxpr/ppermute | solution.py:21
  331.4 13.4 %collective-permute-start.1 = (bf16[48,1792]{1,0:T(8,128)(2,1)S(1)}, bf16[48,1792]{1,0:T(8,128)(2,1)S(1)}, u32[]{:S(2)}, u32[]{:S(2)}) collective-permute-start(bf16[48,1792]{1,0:T(8,128)(2,1)S(1)} %fusion.129), channel_id=1, source_target_pairs={{32,0},{64,32},{96,64},{128,96},{160,128},{192,160},{224,192},{256... | collective-permute-start | bytes 516104 | tf_op jit(solution)/shard_map/while/body/eval_jaxpr/ppermute | solution.py:21
  349.1 13.4 %collective-permute-start.1 = (bf16[48,1792]{1,0:T(8,128)(2,1)S(1)}, bf16[48,1792]{1,0:T(8,128)(2,1)S(1)}, u32[]{:S(2)}, u32[]{:S(2)}) collective-permute-start(bf16[48,1792]{1,0:T(8,128)(2,1)S(1)} %fusion.129), channel_id=1, source_target_pairs={{32,0},{64,32},{96,64},{128,96},{160,128},{192,160},{224,192},{256... | collective-permute-start | bytes 516104 | tf_op jit(solution)/shard_map/while/body/eval_jaxpr/ppermute | solution.py:21
  366.9 13.4 %collective-permute-start.1 = (bf16[48,1792]{1,0:T(8,128)(2,1)S(1)}, bf16[48,1792]{1,0:T(8,128)(2,1)S(1)}, u32[]{:S(2)}, u32[]{:S(2)}) collective-permute-start(bf16[48,1792]{1,0:T(8,128)(2,1)S(1)} %fusion.129), channel_id=1, source_target_pairs={{32,0},{64,32},{96,64},{128,96},{160,128},{192,160},{224,192},{256... | collective-permute-start | bytes 516104 | tf_op jit(solution)/shard_map/while/body/eval_jaxpr/ppermute | solution.py:21
  384.6 13.4 %collective-permute-start.1 = (bf16[48,1792]{1,0:T(8,128)(2,1)S(1)}, bf16[48,1792]{1,0:T(8,128)(2,1)S(1)}, u32[]{:S(2)}, u32[]{:S(2)}) collective-permute-start(bf16[48,1792]{1,0:T(8,128)(2,1)S(1)} %fusion.129), channel_id=1, source_target_pairs={{32,0},{64,32},{96,64},{128,96},{160,128},{192,160},{224,192},{256... | collective-permute-start | bytes 516104 | tf_op jit(solution)/shard_map/while/body/eval_jaxpr/ppermute | solution.py:21
  402.3 13.8 %collective-permute-start.1 = (bf16[48,1792]{1,0:T(8,128)(2,1)S(1)}, bf16[48,1792]{1,0:T(8,128)(2,1)S(1)}, u32[]{:S(2)}, u32[]{:S(2)}) collective-permute-start(bf16[48,1792]{1,0:T(8,128)(2,1)S(1)} %fusion.129), channel_id=1, source_target_pairs={{32,0},{64,32},{96,64},{128,96},{160,128},{192,160},{224,192},{256... | collective-permute-start | bytes 516104 | tf_op jit(solution)/shard_map/while/body/eval_jaxpr/ppermute | solution.py:21
  420.4 14.5 %collective-permute-start.1 = (bf16[48,1792]{1,0:T(8,128)(2,1)S(1)}, bf16[48,1792]{1,0:T(8,128)(2,1)S(1)}, u32[]{:S(2)}, u32[]{:S(2)}) collective-permute-start(bf16[48,1792]{1,0:T(8,128)(2,1)S(1)} %fusion.129), channel_id=1, source_target_pairs={{32,0},{64,32},{96,64},{128,96},{160,128},{192,160},{224,192},{256... | collective-permute-start | bytes 516104 | tf_op jit(solution)/shard_map/while/body/eval_jaxpr/ppermute | solution.py:21
  439.2 14.5 %collective-permute-start.1 = (bf16[48,1792]{1,0:T(8,128)(2,1)S(1)}, bf16[48,1792]{1,0:T(8,128)(2,1)S(1)}, u32[]{:S(2)}, u32[]{:S(2)}) collective-permute-start(bf16[48,1792]{1,0:T(8,128)(2,1)S(1)} %fusion.129), channel_id=1, source_target_pairs={{32,0},{64,32},{96,64},{128,96},{160,128},{192,160},{224,192},{256... | collective-permute-start | bytes 516104 | tf_op jit(solution)/shard_map/while/body/eval_jaxpr/ppermute | solution.py:21
  458.1 14.5 %collective-permute-start.1 = (bf16[48,1792]{1,0:T(8,128)(2,1)S(1)}, bf16[48,1792]{1,0:T(8,128)(2,1)S(1)}, u32[]{:S(2)}, u32[]{:S(2)}) collective-permute-start(bf16[48,1792]{1,0:T(8,128)(2,1)S(1)} %fusion.129), channel_id=1, source_target_pairs={{32,0},{64,32},{96,64},{128,96},{160,128},{192,160},{224,192},{256... | collective-permute-start | bytes 516104 | tf_op jit(solution)/shard_map/while/body/eval_jaxpr/ppermute | solution.py:21
  476.9 14.5 %collective-permute-start.1 = (bf16[48,1792]{1,0:T(8,128)(2,1)S(1)}, bf16[48,1792]{1,0:T(8,128)(2,1)S(1)}, u32[]{:S(2)}, u32[]{:S(2)}) collective-permute-start(bf16[48,1792]{1,0:T(8,128)(2,1)S(1)} %fusion.129), channel_id=1, source_target_pairs={{32,0},{64,32},{96,64},{128,96},{160,128},{192,160},{224,192},{256... | collective-permute-start | bytes 516104 | tf_op jit(solution)/shard_map/while/body/eval_jaxpr/ppermute | solution.py:21
  496.8 13.6 %collective-permute-start.3 = (bf16[48,1792]{1,0:T(8,128)(2,1)S(1)}, bf16[48,1792]{1,0:T(8,128)(2,1)S(1)}, u32[]{:S(2)}, u32[]{:S(2)}) collective-permute-start(bf16[48,1792]{1,0:T(8,128)(2,1)S(1)} %fusion.136), channel_id=1, source_target_pairs={{32,0},{64,32},{96,64},{128,96},{160,128},{192,160},{224,192},{256... | collective-permute-start | bytes 516104 | tf_op jit(solution)/shard_map/while/body/eval_jaxpr/ppermute | solution.py:21
  514.7 14.5 %collective-permute-start.3 = (bf16[48,1792]{1,0:T(8,128)(2,1)S(1)}, bf16[48,1792]{1,0:T(8,128)(2,1)S(1)}, u32[]{:S(2)}, u32[]{:S(2)}) collective-permute-start(bf16[48,1792]{1,0:T(8,128)(2,1)S(1)} %fusion.136), channel_id=1, source_target_pairs={{32,0},{64,32},{96,64},{128,96},{160,128},{192,160},{224,192},{256... | collective-permute-start | bytes 516104 | tf_op jit(solution)/shard_map/while/body/eval_jaxpr/ppermute | solution.py:21
  533.5 14.5 %collective-permute-start.3 = (bf16[48,1792]{1,0:T(8,128)(2,1)S(1)}, bf16[48,1792]{1,0:T(8,128)(2,1)S(1)}, u32[]{:S(2)}, u32[]{:S(2)}) collective-permute-start(bf16[48,1792]{1,0:T(8,128)(2,1)S(1)} %fusion.136), channel_id=1, source_target_pairs={{32,0},{64,32},{96,64},{128,96},{160,128},{192,160},{224,192},{256... | collective-permute-start | bytes 516104 | tf_op jit(solution)/shard_map/while/body/eval_jaxpr/ppermute | solution.py:21
  552.4 14.4 %collective-permute-start.3 = (bf16[48,1792]{1,0:T(8,128)(2,1)S(1)}, bf16[48,1792]{1,0:T(8,128)(2,1)S(1)}, u32[]{:S(2)}, u32[]{:S(2)}) collective-permute-start(bf16[48,1792]{1,0:T(8,128)(2,1)S(1)} %fusion.136), channel_id=1, source_target_pairs={{32,0},{64,32},{96,64},{128,96},{160,128},{192,160},{224,192},{256... | collective-permute-start | bytes 516104 | tf_op jit(solution)/shard_map/while/body/eval_jaxpr/ppermute | solution.py:21
  571.1 14.6 %collective-permute-start.3 = (bf16[48,1792]{1,0:T(8,128)(2,1)S(1)}, bf16[48,1792]{1,0:T(8,128)(2,1)S(1)}, u32[]{:S(2)}, u32[]{:S(2)}) collective-permute-start(bf16[48,1792]{1,0:T(8,128)(2,1)S(1)} %fusion.136), channel_id=1, source_target_pairs={{32,0},{64,32},{96,64},{128,96},{160,128},{192,160},{224,192},{256... | collective-permute-start | bytes 516104 | tf_op jit(solution)/shard_map/while/body/eval_jaxpr/ppermute | solution.py:21
  590.1 14.5 %collective-permute-start.3 = (bf16[48,1792]{1,0:T(8,128)(2,1)S(1)}, bf16[48,1792]{1,0:T(8,128)(2,1)S(1)}, u32[]{:S(2)}, u32[]{:S(2)}) collective-permute-start(bf16[48,1792]{1,0:T(8,128)(2,1)S(1)} %fusion.136), channel_id=1, source_target_pairs={{32,0},{64,32},{96,64},{128,96},{160,128},{192,160},{224,192},{256... | collective-permute-start | bytes 516104 | tf_op jit(solution)/shard_map/while/body/eval_jaxpr/ppermute | solution.py:21
  608.9 14.5 %collective-permute-start.3 = (bf16[48,1792]{1,0:T(8,128)(2,1)S(1)}, bf16[48,1792]{1,0:T(8,128)(2,1)S(1)}, u32[]{:S(2)}, u32[]{:S(2)}) collective-permute-start(bf16[48,1792]{1,0:T(8,128)(2,1)S(1)} %fusion.136), channel_id=1, source_target_pairs={{32,0},{64,32},{96,64},{128,96},{160,128},{192,160},{224,192},{256... | collective-permute-start | bytes 516104 | tf_op jit(solution)/shard_map/while/body/eval_jaxpr/ppermute | solution.py:21
  627.8 14.5 %collective-permute-start.3 = (bf16[48,1792]{1,0:T(8,128)(2,1)S(1)}, bf16[48,1792]{1,0:T(8,128)(2,1)S(1)}, u32[]{:S(2)}, u32[]{:S(2)}) collective-permute-start(bf16[48,1792]{1,0:T(8,128)(2,1)S(1)} %fusion.136), channel_id=1, source_target_pairs={{32,0},{64,32},{96,64},{128,96},{160,128},{192,160},{224,192},{256... | collective-permute-start | bytes 516104 | tf_op jit(solution)/shard_map/while/body/eval_jaxpr/ppermute | solution.py:21
  646.6 14.5 %collective-permute-start.3 = (bf16[48,1792]{1,0:T(8,128)(2,1)S(1)}, bf16[48,1792]{1,0:T(8,128)(2,1)S(1)}, u32[]{:S(2)}, u32[]{:S(2)}) collective-permute-start(bf16[48,1792]{1,0:T(8,128)(2,1)S(1)} %fusion.136), channel_id=1, source_target_pairs={{32,0},{64,32},{96,64},{128,96},{160,128},{192,160},{224,192},{256... | collective-permute-start | bytes 516104 | tf_op jit(solution)/shard_map/while/body/eval_jaxpr/ppermute | solution.py:21
  665.4 14.5 %collective-permute-start.3 = (bf16[48,1792]{1,0:T(8,128)(2,1)S(1)}, bf16[48,1792]{1,0:T(8,128)(2,1)S(1)}, u32[]{:S(2)}, u32[]{:S(2)}) collective-permute-start(bf16[48,1792]{1,0:T(8,128)(2,1)S(1)} %fusion.136), channel_id=1, source_target_pairs={{32,0},{64,32},{96,64},{128,96},{160,128},{192,160},{224,192},{256... | collective-permute-start | bytes 516104 | tf_op jit(solution)/shard_map/while/body/eval_jaxpr/ppermute | solution.py:21
  684.3 14.5 %collective-permute-start.3 = (bf16[48,1792]{1,0:T(8,128)(2,1)S(1)}, bf16[48,1792]{1,0:T(8,128)(2,1)S(1)}, u32[]{:S(2)}, u32[]{:S(2)}) collective-permute-start(bf16[48,1792]{1,0:T(8,128)(2,1)S(1)} %fusion.136), channel_id=1, source_target_pairs={{32,0},{64,32},{96,64},{128,96},{160,128},{192,160},{224,192},{256... | collective-permute-start | bytes 516104 | tf_op jit(solution)/shard_map/while/body/eval_jaxpr/ppermute | solution.py:21
  (113 other events, 613.0 us)
Sparse Core Ops, SparseCore 0:
  703.7 88.2 reduce-scatter.1
where the time goes:
time: 911 us; the launch traced here: 906 us
  starting transfers between devices  338 us (37%)
  waiting for transfers between devices  173 us (19%)
  other arithmetic  130 us (14%)
  blocking collectives  125 us (14%)
  local copies, waits for them, and re-layouts  75.4 us (8%)
  matrix products  40.2 us (4%)
  between operations  16.9 us (2%)
    ppermute x70, starting transfers between devices, from_behind(): return lax.ppermute(block, axis, route)  295 us
    psum x1, blocking collectives, shards(): total = lax.psum(local_squares, ('section', 'tp', 'dp'))  102 us
    ppermute x70, waiting for transfers between devices, from_behind(): return lax.ppermute(block, axis, route)  80.5 us
    dynamic_update_slice x70, other arithmetic, keep_slot(): lax.dynamic_update_index_in_dim(buffer, jnp.where(active, value, previous...  71.3 us
    reduce_scatter x1, waiting for transfers between devices, shards(): lax.psum_scatter(mix_local, 'dp', scatter_dimension=1, tiled=True)  64 us
    ppermute x8, starting transfers between devices, swapped(): lax.ppermute(x, axis, [(i, i ^ 1 << apart) for i in range(lax.axis_size(a...  42.6 us
    ppermute x8, waiting for transfers between devices, swapped(): lax.ppermute(x, axis, [(i, i ^ 1 << apart) for i in range(lax.axis_size(a...  28.8 us
    while x194, local copies, waits for them, and re-layouts  23.5 us
  transfers between devices with their start and end apart: 79, of which 43 were waited for; matrix products, arithmetic and copies ran while one was open for 20% of the time, Pallas kernels for 0%

commit v1 on v0

v1 whole, which is shorter than its diff:
```python
import functools
import math

import jax
import jax.numpy as jnp
from jax import lax
from jax.experimental import pallas as pl
from jax.experimental.pallas import tpu as pltpu
from jax.sharding import PartitionSpec as P

EPSILON = 1e-05
GRAD_EPS = 1e-06
GELU_K = math.sqrt(2.0 / math.pi)
GELU_C = 0.044715


def forward_layer(wide, gain, bias, weights):
    mean = jnp.mean(wide, axis=-1, keepdims=True)
    centred = wide - mean
    inv_std = lax.rsqrt(jnp.mean(centred * centred, axis=-1, keepdims=True) + EPSILON)
    normed = centred * inv_std
    pre = normed * gain + bias
    square = pre * pre
    tangent = jnp.tanh(pre * (GELU_K + (GELU_K * GELU_C) * square))
    half = 0.5 + 0.5 * tangent
    act = pre * half
    slope = half + act * (1.0 - tangent) * (GELU_K + (3.0 * GELU_K * GELU_C) * square)
    act = act.astype(jnp.bfloat16)
    mixed = jnp.dot(act, weights, preferred_element_type=jnp.float32)
    return (wide + mixed).astype(jnp.bfloat16), normed, inv_std, act, slope


def backward_layer(grad, normed, inv_std, act, slope, gain, weights):
    grad_act = lax.dot_general(
        grad, weights, (((1,), (1,)), ((), ())), preferred_element_type=jnp.float32
    )
    mix_part = lax.dot_general(
        act, grad, (((0,), (0,)), ((), ())), preferred_element_type=jnp.float32
    )
    grad_pre = grad_act * slope
    gain_term = grad_pre * normed
    grad_norm = grad_pre * gain
    first = jnp.mean(grad_norm, axis=-1, keepdims=True)
    second = jnp.mean(gain_term * gain, axis=-1, keepdims=True)
    grad_in = grad.astype(jnp.float32) + inv_std * (grad_norm - first - normed * second)
    gain_part = jnp.sum(gain_term, axis=0, keepdims=True)
    bias_part = jnp.sum(grad_pre, axis=0, keepdims=True)
    return grad_in.astype(jnp.bfloat16), mix_part, gain_part, bias_part


def stack_kernel(
    loss_scale, x_ref, params_ref, weights_ref, mix_ref, vec_ref, flow, normed_s, inv_s, act_s, slope_s
):
    layers = weights_ref.shape[0]
    flow[...] = x_ref[...]

    @pl.loop(0, layers)
    def _(layer):
        wide = flow[...].astype(jnp.float32)
        out, normed, inv_std, act, slope = forward_layer(
            wide, params_ref[layer, 0:1], params_ref[layer, 1:2], weights_ref[layer]
        )
        flow[...] = out
        normed_s[layer] = normed
        inv_s[layer] = jnp.broadcast_to(inv_std, normed.shape)
        act_s[layer] = act
        slope_s[layer] = slope

    flow[...] = (flow[...].astype(jnp.float32) * loss_scale).astype(jnp.bfloat16)

    @pl.loop(0, layers)
    def _(step):
        layer = layers - 1 - step
        grad_in, mix_part, gain_part, bias_part = backward_layer(
            flow[...],
            normed_s[layer],
            inv_s[layer],
            act_s[layer],
            slope_s[layer],
            params_ref[layer, 0:1],
            weights_ref[layer],
        )
        flow[...] = grad_in
        mix_ref[layer] = mix_part
        vec_ref[layer, 0:1] = gain_part
        vec_ref[layer, 1:2] = bias_part


def run_stack(x, params, weights, loss_scale):
    layers = weights.shape[0]
    rows, size = x.shape
    return pl.pallas_call(
        functools.partial(stack_kernel, loss_scale),
        out_shape=(
            jax.ShapeDtypeStruct((layers, size, size), jnp.float32),
            jax.ShapeDtypeStruct((layers, 2, size), jnp.float32),
        ),
        in_specs=[pl.BlockSpec(memory_space=pltpu.VMEM)] * 3,
        out_specs=[pl.BlockSpec(memory_space=pltpu.VMEM)] * 2,
        scratch_shapes=[
            pltpu.VMEM((rows, size), jnp.bfloat16),
            pltpu.VMEM((layers, rows, size), jnp.float32),
            pltpu.VMEM((layers, rows, size), jnp.float32),
            pltpu.VMEM((layers, rows, size), jnp.bfloat16),
            pltpu.VMEM((layers, rows, size), jnp.float32),
        ],
        compiler_params=pltpu.CompilerParams(vmem_limit_bytes=32 << 20),
        name="stack",
    )(x, params, weights)


def shards(inputs, norm_gain, norm_bias, mix):
    sections = lax.axis_size("section")
    me = lax.axis_index("section")
    batches, rows, features = inputs.shape
    heads, size = mix.shape[1], mix.shape[2]
    feature_total = features * lax.axis_size("tp")
    param_count = sections * (
        2 * feature_total + heads * lax.axis_size("tp") * size * size
    )
    loss_scale = 1.0 / math.sqrt(batches * rows * lax.axis_size("dp"))
    head = jnp.minimum(me, heads - 1)
    x = lax.dynamic_slice_in_dim(inputs, head * size, size, 2).reshape(batches * rows, size)
    params = jnp.stack([norm_gain.reshape(heads, size), norm_bias.reshape(heads, size)], 1)
    spare = sections - heads
    params = jnp.pad(params, ((0, spare), (0, 0), (0, 0)))
    weights = jnp.pad(mix[0], ((0, spare), (0, 0), (0, 0)))
    params = lax.all_to_all(params, "section", 0, 0, tiled=True)
    weights = lax.all_to_all(weights, "section", 0, 0, tiled=True)
    mix_part, vec_part = run_stack(x, params, weights, loss_scale)
    mix_sum = lax.psum_scatter(mix_part, "dp", scatter_dimension=1, tiled=True)
    vec_sum = lax.psum(vec_part, "dp")
    mix_sum = lax.all_to_all(mix_sum, "section", 0, 0, tiled=True)[:heads]
    vec_sum = lax.all_to_all(vec_sum, "section", 0, 0, tiled=True)[:heads]
    squares = jnp.sum(mix_sum * mix_sum) + jnp.sum(vec_sum * vec_sum) / lax.axis_size("dp")
    total = lax.psum(squares, ("section", "tp", "dp"))
    scale = lax.rsqrt(total / param_count + GRAD_EPS)
    vec_sum = vec_sum * scale
    return (
        vec_sum[:, 0].reshape(1, features),
        vec_sum[:, 1].reshape(1, features),
        (mix_sum * scale)[None],
    )


def solution(mesh):
    placed = (
        P(None, "dp", "tp"),
        P("section", "tp"),
        P("section", "tp"),
        P("section", "tp", None, None),
    )
    return jax.shard_map(
        shards,
        mesh=mesh,
        in_specs=placed,
        out_specs=(P("section", "tp"), P("section", "tp"), P("section", "tp", "dp", None)),
        check_vma=False,
    )
```

time: 911 us -> 218 us (0.24)
  starting transfers between devices: 338 us -> 21 us
  waiting for transfers between devices: 173 us -> 30.5 us
  other arithmetic: 130 us -> 3.3 us
  local copies, waits for them, and re-layouts: 75.4 us -> 2.49 us
  matrix products: 40.2 us -> 0 us
  Pallas kernels: 0 us -> 11.1 us
    ppermute x78 -> x0, starting transfers between devices: 338 us -> none  [the longest x70 295 us: from_behind(): return lax.ppermute(block, axis, route)]
    ppermute x78 -> x0, waiting for transfers between devices: 109 us -> none  [the longest x70 80.5 us: from_behind(): return lax.ppermute(block, axis, route)]
    dynamic_update_slice x70 -> x0, other arithmetic: 71.3 us -> none  [keep_slot(): lax.dynamic_update_index_in_dim(buffer, jnp.where(active, value, previous...]
    reduce_scatter x1, waiting for transfers between devices: 64 us -> 4.2 us  [shards(): mix_sum = lax.psum_scatter(mix_part, 'dp', scatter_dimension=1, tiled=True)]
    dot_general x71 -> x0, matrix products: 40.2 us -> none  [the longest x35 23.2 us: one_tick(): jnp.einsum('rhj,hkj->rhk', grad_out.reshape(row_count, head_count, head_s...]
    reduce_sum x142 -> x2, other arithmetic: 35.9 us -> 1.24 us  [the longest x1 0.63 us: shards(): jnp.sum(mix_sum * mix_sum)]
    all_to_all x0 -> x3, waiting for transfers between devices: none -> 26.3 us  [the longest x1 15.4 us: shards(): weights = lax.all_to_all(weights, 'section', 0, 0, tiled=True)]
    while x194 -> x0, local copies, waits for them, and re-layouts: 23.5 us -> none
  transfers between devices with their start and end apart: 79 -> 4, of which waited for: 43 -> 4; matrix products, arithmetic and copies ran while one was open for 20% -> 1% of each run, Pallas kernels for 0% -> 0%
where the time goes in v1:
time: 218 us; the launch traced here: 217 us
  blocking collectives  133 us (61%)
  waiting for transfers between devices  30.5 us (14%)
  starting transfers between devices  21 us (10%)
  between operations  16.1 us (7%)
  Pallas kernels  11.1 us (5%)
  other arithmetic  3.3 us (2%)
  local copies, waits for them, and re-layouts  2.49 us (1%)
    psum x1, blocking collectives, shards(): total = lax.psum(squares, ('section', 'tp', 'dp'))  99.2 us
    psum x1, blocking collectives, shards(): vec_sum = lax.psum(vec_part, 'dp')  23.6 us
    all_to_all x1, waiting for transfers between devices, shards(): weights = lax.all_to_all(weights, 'section', 0, 0, tiled=True)  15.4 us
    pallas_call x1, Pallas kernels, run_stack(): pl.pallas_call(functools.partial(stack_kernel, loss_scale), out_shape=(ja...  11.1 us
    all_to_all x1, starting transfers between devices, shards(): params = lax.all_to_all(params, 'section', 0, 0, tiled=True)  10.4 us
    all_to_all x1, blocking collectives, shards(): vec_sum = lax.all_to_all(vec_sum, 'section', 0, 0, tiled=True)[:heads]  9.98 us
    all_to_all x1, starting transfers between devices, shards(): mix_sum = lax.all_to_all(mix_sum, 'section', 0, 0, tiled=True)[:heads]  6.97 us
    all_to_all x1, waiting for transfers between devices, shards(): mix_sum = lax.all_to_all(mix_sum, 'section', 0, 0, tiled=True)[:heads]  5.98 us
  transfers between devices with their start and end apart: 4, of which 4 were waited for; matrix products, arithmetic and copies ran while one was open for 1% of the time, Pallas kernels for 0%

profile of v1, /device:TPU:1, one launch (start us, length us, event | category | flops | bytes accessed | tf_op | source)
XLA Modules:
  0.0 217.3 jit_solution(6745017658065490064)
XLA Ops:
  7.2 0.0 copy-start
  7.2 1.4 select_maximum_fusion
  8.6 10.4 %all-to-all-start = ((f32[16,2,128]{2,1,0:T(2,128)}), f32[16,2,128]{2,1,0:T(2,128)S(1)}, u32[]{:S(2)}, u32[]{:S(2)}) async-start(f32[16,2,128]{2,1,0:T(2,128)} %select_maximum_fusion), calls=%async_computation | async-start | bytes 32768 | tf_op jit(solution)/shard_map/all_to_all | solution.py:128
  19.0 1.9 pad.9
  20.8 4.9 %all-to-all-done.params_ref = f32[16,2,128]{2,1,0:T(2,128)S(1)} async-done(((f32[16,2,128]{2,1,0:T(2,128)}), f32[16,2,128]{2,1,0:T(2,128)S(1)}, u32[]{:S(2)}, u32[]{:S(2)}) %all-to-all-start) | async-done | bytes 16416 | tf_op jit(solution)/shard_map/all_to_all | solution.py:128
  25.8 3.6 %all-to-all-start.1 = ((bf16[16,128,128]{2,1,0:T(8,128)(2,1)}), bf16[16,128,128]{2,1,0:T(8,128)(2,1)S(1)}, u32[]{:S(2)}, u32[]{:S(2)}) async-start(bf16[16,128,128]{2,1,0:T(8,128)(2,1)} %pad.9), calls=%async_computation.1 | async-start | bytes 1048576 | tf_op jit(solution)/shard_map/all_to_all | solution.py:129
  29.3 0.0 reduce-scatter.2.cloned.1.call-start
  29.4 0.0 copy-done
  29.4 15.4 %all-to-all-done.1.weights_ref = bf16[16,128,128]{2,1,0:T(8,128)(2,1)S(1)} async-done(((bf16[16,128,128]{2,1,0:T(8,128)(2,1)}), bf16[16,128,128]{2,1,0:T(8,128)(2,1)S(1)}, u32[]{:S(2)}, u32[]{:S(2)}) %all-to-all-start.1) | async-done | bytes 524320 | tf_op jit(solution)/shard_map/all_to_all | solution.py:129
  44.8 11.1 %stack.5 = (f32[16,128,128]{2,1,0:T(8,128)}, f32[16,2,128]{2,1,0:T(2,128)S(1)}) custom-call(bf16[192,128]{1,0:T(8,128)(2,1)S(1)} %bitcast.10, f32[16,2,128]{2,1,0:T(2,128)S(1)} %all-to-all-done.params_ref, bf16[16,128,128]{2,1,0:T(8,128)(2,1)S(1)} %all-to-all-done.1.weights_ref), custom_call_target="tpu_custom_call" | custom-call | tf_op jit(solution)/shard_map/stack/pallas_call | solution.py:92
  56.0 0.0 reduce-scatter.2.cloned.1.call-update
  56.0 23.6 %psum.14 = f32[16,2,128]{2,1,0:T(2,128)S(1)} all-reduce(f32[16,2,128]{2,1,0:T(2,128)S(1)} %get-tuple-element.5), channel_id=1, replica_groups=mesh['section'=16,'tp'=4,'dp'=8] {'dp'}, use_global_device_ids=true, to_apply=%region_0.1 | all-reduce | flops 4096 | bytes 32768 | tf_op jit(solution)/shard_map/psum | solution.py:132
  79.6 10.0 %all_to_all.20 = f32[16,2,128]{2,1,0:T(2,128)S(1)} all-to-all(f32[16,2,128]{2,1,0:T(2,128)S(1)} %psum.14), channel_id=1, replica_groups=mesh['section'=16,'tp'=4,'dp'=8] {'section'}, dimensions={0} | all-to-all | bytes 32768 | tf_op jit(solution)/shard_map/all_to_all | solution.py:134
  89.6 4.2 %reduce-scatter.2.cloned.1.call-done = f32[16,16,128]{2,1,0:T(8,128)} async-done(((f32[16,128,128]{2,1,0:T(8,128)}), f32[16,16,128]{2,1,0:T(8,128)}) %reduce-scatter.2.cloned.1.call-update) | async-done | bytes 131088 | tf_op jit(solution)/shard_map/reduce_scatter | solution.py:131
  93.8 7.0 %all-to-all-start.3 = ((f32[16,16,128]{2,1,0:T(8,128)}), f32[16,16,128]{2,1,0:T(8,128)S(1)}, u32[]{:S(2)}, u32[]{:S(2)}) async-start(f32[16,16,128]{2,1,0:T(8,128)} %reduce-scatter.2.cloned.1.call-done), calls=%async_computation.4 | async-start | bytes 262144 | tf_op jit(solution)/shard_map/all_to_all | solution.py:133
  100.7 0.6 multiply_reduce_fusion.1
  102.0 6.0 %all-to-all-done.3 = f32[16,16,128]{2,1,0:T(8,128)S(1)} async-done(((f32[16,16,128]{2,1,0:T(8,128)}), f32[16,16,128]{2,1,0:T(8,128)S(1)}, u32[]{:S(2)}, u32[]{:S(2)}) %all-to-all-start.3) | async-done | bytes 131104 | tf_op jit(solution)/shard_map/all_to_all | solution.py:133
  108.0 0.6 multiply_reduce_fusion
  109.3 99.2 %psum.15 = f32[]{:T(128)} all-reduce(f32[]{:T(128)S(6)} %add.20), channel_id=1, replica_groups=mesh['section'=16,'tp'=4,'dp'=8] {'section','tp','dp'}, use_global_device_ids=true, to_apply=%region_4.5 | all-reduce | flops 1 | bytes 8 | tf_op jit(solution)/shard_map/psum | solution.py:136
  209.2 0.6 slice_bitcast_fusion
  209.8 0.7 multiply_bitcast_fusion
  (2 shorter events, 0.0 us)
Async XLA Ops:
  7.2 22.2 %copy-start = (bf16[4,48,1792]{2,1,0:T(8,128)(2,1)S(1)}, bf16[4,48,1792]{2,1,0:T(8,128)(2,1)}, u32[]{:S(2)}) copy-start(bf16[4,48,1792]{2,1,0:T(8,128)(2,1)} %param.4) | copy-start | bytes 2064388
  8.6 17.2 %all-to-all-start = ((f32[16,2,128]{2,1,0:T(2,128)}), f32[16,2,128]{2,1,0:T(2,128)S(1)}, u32[]{:S(2)}, u32[]{:S(2)}) async-start(f32[16,2,128]{2,1,0:T(2,128)} %select_maximum_fusion), calls=%async_computation | async-start | bytes 32768 | tf_op jit(solution)/shard_map/all_to_all | solution.py:128
  25.8 19.1 %all-to-all-start.1 = ((bf16[16,128,128]{2,1,0:T(8,128)(2,1)}), bf16[16,128,128]{2,1,0:T(8,128)(2,1)S(1)}, u32[]{:S(2)}, u32[]{:S(2)}) async-start(bf16[16,128,128]{2,1,0:T(8,128)(2,1)} %pad.9), calls=%async_computation.1 | async-start | bytes 1048576 | tf_op jit(solution)/shard_map/all_to_all | solution.py:129
  29.3 64.4 %reduce-scatter.2.cloned.1.call-start = ((), (), s32[]{:S(2)}) async-start(), calls=%async_computation.5 | async-start | bytes 1179648 | tf_op jit(solution)/shard_map/reduce_scatter | solution.py:131
  93.8 14.2 %all-to-all-start.3 = ((f32[16,16,128]{2,1,0:T(8,128)}), f32[16,16,128]{2,1,0:T(8,128)S(1)}, u32[]{:S(2)}, u32[]{:S(2)}) async-start(f32[16,16,128]{2,1,0:T(8,128)} %reduce-scatter.2.cloned.1.call-done), calls=%async_computation.4 | async-start | bytes 262144 | tf_op jit(solution)/shard_map/all_to_all | solution.py:133
Sparse Core Ops, SparseCore 0:
  56.1 37.6 reduce-scatter.1

commit v2 on v1

v2 whole, which is shorter than its diff:
```python
import functools
import math

import jax
import jax.numpy as jnp
from jax import lax
from jax.experimental import pallas as pl
from jax.experimental.pallas import tpu as pltpu
from jax.sharding import PartitionSpec as P

EPSILON = 1e-05
GRAD_EPS = 1e-06
GELU_K = math.sqrt(2.0 / math.pi)
GELU_C = 0.044715


def forward_layer(wide, gain, bias, weights):
    mean = jnp.mean(wide, axis=-1, keepdims=True)
    centred = wide - mean
    inv_std = lax.rsqrt(jnp.mean(centred * centred, axis=-1, keepdims=True) + EPSILON)
    normed = centred * inv_std
    pre = normed * gain + bias
    square = pre * pre
    tangent = jnp.tanh(pre * (GELU_K + (GELU_K * GELU_C) * square))
    half = 0.5 + 0.5 * tangent
    act = pre * half
    slope = half + act * (1.0 - tangent) * (GELU_K + (3.0 * GELU_K * GELU_C) * square)
    act = act.astype(jnp.bfloat16)
    mixed = jnp.dot(act, weights, preferred_element_type=jnp.float32)
    return (wide + mixed).astype(jnp.bfloat16), normed, inv_std, act, slope


def backward_layer(grad, normed, inv_std, act, slope, gain, weights):
    grad_act = lax.dot_general(
        grad, weights, (((1,), (1,)), ((), ())), preferred_element_type=jnp.float32
    )
    mix_part = lax.dot_general(
        act, grad, (((0,), (0,)), ((), ())), preferred_element_type=jnp.float32
    )
    grad_pre = grad_act * slope
    gain_term = grad_pre * normed
    grad_norm = grad_pre * gain
    first = jnp.mean(grad_norm, axis=-1, keepdims=True)
    second = jnp.mean(gain_term * gain, axis=-1, keepdims=True)
    grad_in = grad.astype(jnp.float32) + inv_std * (grad_norm - first - normed * second)
    gain_part = jnp.sum(gain_term, axis=0, keepdims=True)
    bias_part = jnp.sum(grad_pre, axis=0, keepdims=True)
    return grad_in.astype(jnp.bfloat16), mix_part, gain_part, bias_part


MESH = pl.DeviceIdType.MESH
LAG = 3
AHEAD = 2


def relay_kernel(
    loss_scale,
    param_count,
    x_ref,
    gain_ref,
    bias_ref,
    mix_ref,
    raw_ref,
    scale_ref,
    x_in,
    stage,
    params,
    weights,
    flow,
    normed_s,
    inv_s,
    act_s,
    slope_s,
    part_mix,
    part_vec,
    out1,
    out2,
    out3,
    out4,
    in1,
    in2,
    in3,
    in4,
    square,
    all_dp,
    all_section,
    all_tp,
    x_sent,
    x_came,
    w_sent,
    w_came,
    p_sent,
    p_came,
    f_sent,
    f_came,
    sent1,
    sent2,
    sent3,
    sent4,
    came1,
    came2,
    came3,
    came4,
    dp_sent,
    dp_came,
    section_sent,
    section_came,
    tp_sent,
    tp_came,
):
    section, tp, dp = (lax.axis_index(name) for name in ("section", "tp", "dp"))
    layers = weights.shape[0]
    heads = mix_ref.shape[0]
    size = mix_ref.shape[1]
    half, quarter, eighth = size // 2, size // 4, size // 8
    pairs = lax.axis_size("dp") // 2
    core, high = lax.rem(tp, 2), lax.div(tp, 2)
    unit, z_bit = lax.div(section, 2), lax.rem(section, 2)
    pair, y_bit = lax.div(dp, 2), lax.rem(dp, 2)
    place = unit * pairs + pair
    kin = lax.div(place, heads)
    head = place - kin * heads
    active = place < 2 * heads
    owner_tp = high * 2 + kin
    part = core * 4 + y_bit * 2 + z_bit

    def remote(source, target, sent, came, **where):
        return pltpu.make_async_remote_copy(
            src_ref=source,
            dst_ref=target,
            send_sem=sent,
            recv_sem=came,
            device_id=where,
            device_id_type=MESH,
        )

    def send(is_here, source, target, sent, came, **where):
        @pl.when(is_here)
        def _():
            pltpu.make_async_copy(source, target, came).start()

        @pl.when(jnp.logical_not(is_here))
        def _():
            remote(source, target, sent, came, **where).start()

    def x_plan(other_pair):
        here = unit * pairs + other_pair
        goes = (lax.div(here, heads) == core) & (y_bit == z_bit)
        to_dp = other_pair * 2 + lax.rem(pair, 2)
        to_core = lax.div(dp, 4)
        mine = (to_dp == dp) & (to_core == core)
        return here - core * heads, goes, mine, to_dp, high * 2 + to_core

    for other_pair in range(pairs):
        item, goes, mine, to_dp, to_tp = x_plan(other_pair)

        @pl.when(goes)
        def _():
            columns = pl.ds(pl.multiple_of(item * size, size), size)
            send(
                mine,
                x_ref.at[:, :, columns],
                x_in,
                x_sent.at[other_pair],
                x_came,
                tp=to_tp,
                dp=to_dp,
            )

    for item in range(heads):
        columns = slice(item * size, (item + 1) * size)
        stage[item, 0:1] = gain_ref[0:1, columns]
        stage[item, 1:2] = bias_ref[0:1, columns]
    part_vec[...] = jnp.zeros_like(part_vec)
    square[...] = jnp.zeros_like(square)
    middle = lax.div(heads + pairs - 1 - pair, pairs)
    stop = lax.div(2 * heads + pairs - 1 - pair, pairs)
    low = jnp.where(core == 0, 0, middle)
    high_end = jnp.where(core == 0, middle, stop)

    @pl.loop(low, high_end)
    def _(to_unit):
        item = to_unit * pairs + pair - core * heads
        for bit in range(2):
            to_section = to_unit * 2 + bit
            for to_core in range(2):
                mine = (to_section == section) & (core == to_core)
                rows = pl.ds(to_core * half, half)
                to_tp = high * 2 + to_core
                send(
                    mine,
                    stage.at[item],
                    params.at[section],
                    p_sent.at[to_section, to_core],
                    p_came.at[section],
                    section=to_section,
                    tp=to_tp,
                )
                send(
                    mine,
                    mix_ref.at[item, rows],
                    weights.at[section, rows],
                    w_sent.at[to_section, to_core],
                    w_came.at[section],
                    section=to_section,
                    tp=to_tp,
                )

    sibling = high * 2 + 1 - core
    own_rows = pl.ds(pl.multiple_of(core * half, half), half)
    other_rows = pl.ds(pl.multiple_of((1 - core) * half, half), half)

    def forward_half(layer):
        own = weights.at[layer, own_rows]
        return remote(own, own, f_sent.at[layer], f_came.at[layer], tp=sibling)

    def pass_on(layer):
        own = weights.at[layer, own_rows]
        remote(own, own, w_sent.at[0, 0], w_came.at[layer], tp=sibling).wait_recv()
        forward_half(layer).start()

    def exchange1(layer):
        return remote(
            out1.at[layer], in1.at[layer], sent1.at[layer], came1.at[layer], tp=sibling
        )

    def exchange2(layer):
        return remote(
            out2.at[layer],
            in2.at[layer],
            sent2.at[layer],
            came2.at[layer],
            dp=pair * 2 + 1 - y_bit,
        )

    def exchange3(layer):
        return remote(
            out3.at[layer],
            in3.at[layer],
            sent3.at[layer],
            came3.at[layer],
            section=unit * 2 + 1 - z_bit,
        )

    def to_owner(layer):
        return remote(
            out4.at[layer],
            in4.at[head],
            sent4.at[layer],
            came4.at[head],
            section=layer,
            tp=owner_tp,
            dp=part,
        )

    def is_owner(layer):
        return (layer == section) & (owner_tp == tp) & (part == dp)

    def rows_of(ref, layer, start, count):
        return ref[layer, pl.ds(pl.multiple_of(start, 8), count)]

    @pl.when(active)
    def _():
        remote(x_in, x_in, x_sent.at[0], x_came, tp=sibling).wait_recv()
        flow[...] = x_in[...].reshape(flow.shape)
        for layer in range(AHEAD):
            pass_on(layer)

        @pl.loop(0, layers)
        def _(layer):
            @pl.when(layer + AHEAD < layers)
            def _():
                pass_on(layer + AHEAD)

            remote(
                stage.at[0], params.at[layer], p_sent.at[0, 0], p_came.at[layer], tp=sibling
            ).wait_recv()
            theirs = weights.at[layer, other_rows]
            remote(theirs, theirs, f_sent.at[layer], f_came.at[layer], tp=sibling).wait_recv()
            wide = flow[...].astype(jnp.float32)
            out, normed, inv_std, act, slope = forward_layer(
                wide, params[layer, 0:1], params[layer, 1:2], weights[layer]
            )
            flow[...] = out
            normed_s[layer] = normed
            inv_s[layer] = jnp.broadcast_to(inv_std, normed.shape)
            act_s[layer] = act
            slope_s[layer] = slope

        flow[...] = (flow[...].astype(jnp.float32) * loss_scale).astype(jnp.bfloat16)

        @pl.loop(0, layers + 3 * LAG)
        def _(tick):
            @pl.when(tick < layers)
            def _():
                layer = layers - 1 - tick
                grad_in, mix_part, gain_part, bias_part = backward_layer(
                    flow[...],
                    normed_s[layer],
                    inv_s[layer],
                    act_s[layer],
                    slope_s[layer],
                    params[layer, 0:1],
                    weights[layer],
                )
                flow[...] = grad_in
                part_mix[layer] = mix_part
                part_vec[layer, 0:1] = gain_part
                part_vec[layer, 1:2] = bias_part
                out1[layer, 0:half] = rows_of(part_mix, layer, (1 - core) * half, half)
                out1[layer, half:] = part_vec[layer]
                exchange1(layer).start()

            step2 = tick - LAG

            @pl.when((step2 >= 0) & (step2 < layers))
            def _():
                layer = layers - 1 - step2
                exchange1(layer).wait_recv()
                away = (1 - y_bit) * quarter
                out2[layer, 0:quarter] = rows_of(
                    part_mix, layer, core * half + away, quarter
                ) + rows_of(in1, layer, away, quarter)
                out2[layer, quarter:] = part_vec[layer] + in1[layer, half:]
                exchange2(layer).start()

            step3 = tick - 2 * LAG

            @pl.when((step3 >= 0) & (step3 < layers))
            def _():
                layer = layers - 1 - step3
                exchange2(layer).wait_recv()
                away = (1 - z_bit) * eighth
                out3[layer, 0:eighth] = (
                    rows_of(part_mix, layer, core * half + y_bit * quarter + away, eighth)
                    + rows_of(in1, layer, y_bit * quarter + away, eighth)
                ) + rows_of(in2, layer, away, eighth)
                out3[layer, eighth:] = (part_vec[layer] + in1[layer, half:]) + in2[
                    layer, quarter:
                ]
                exchange3(layer).start()

            step4 = tick - 3 * LAG

            @pl.when((step4 >= 0) & (step4 < layers))
            def _():
                layer = layers - 1 - step4
                exchange3(layer).wait_recv()
                mix_sum = (
                    (
                        rows_of(part_mix, layer, part * eighth, eighth)
                        + rows_of(in1, layer, y_bit * quarter + z_bit * eighth, eighth)
                    )
                    + rows_of(in2, layer, z_bit * eighth, eighth)
                ) + in3[layer, 0:eighth]
                vec_sum = (
                    (part_vec[layer] + in1[layer, half:]) + in2[layer, quarter:]
                ) + in3[layer, eighth:]
                out4[layer, 0:eighth] = mix_sum
                out4[layer, eighth:] = vec_sum

                @pl.when(is_owner(layer))
                def _():
                    pltpu.make_async_copy(out4.at[layer], in4.at[head], came4.at[head]).start()

                @pl.when(jnp.logical_not(is_owner(layer)))
                def _():
                    to_owner(layer).start()

                square[0] += jnp.sum(mix_sum * mix_sum, axis=0, keepdims=True) + (
                    1.0 / lax.axis_size("dp")
                ) * jnp.sum(vec_sum * vec_sum, axis=0, keepdims=True)

    stages = (
        ("dp", dp, all_dp, dp_sent, dp_came),
        ("section", section, all_section, section_sent, section_came),
        ("tp", tp, all_tp, tp_sent, tp_came),
    )
    for index, (name, me, slots, sent, came) in enumerate(stages):
        count = lax.axis_size(name)

        def copy_to(peer, index=index, name=name, me=me, slots=slots, sent=sent, came=came):
            return remote(
                square.at[index], slots.at[me], sent.at[peer], came.at[me], **{name: peer}
            )

        def copy_from(peer, index=index, name=name, slots=slots, sent=sent, came=came):
            return remote(
                square.at[index], slots.at[peer], sent.at[peer], came.at[peer], **{name: peer}
            )

        slots[me] = square[index]

        @pl.loop(1, count)
        def _(step):
            copy_to(lax.rem(me + step, count)).start()

        @pl.loop(1, count)
        def _(step):
            copy_from(lax.rem(me + step, count)).wait_recv()

        square[index + 1] = jnp.sum(slots[...], axis=0)

        @pl.loop(1, count)
        def _(step):
            copy_to(lax.rem(me + step, count)).wait_send()

    total = jnp.sum(square[3], axis=-1, keepdims=True)
    scale_ref[...] = jnp.broadcast_to(lax.rsqrt(total / param_count + GRAD_EPS), scale_ref.shape)

    @pl.loop(0, heads)
    def _(item):
        remote(out4.at[0], in4.at[item], sent4.at[0], came4.at[item], tp=sibling).wait_recv()

    raw_ref[...] = in4[...]

    for other_pair in range(pairs):
        item, goes, mine, to_dp, to_tp = x_plan(other_pair)

        @pl.when(goes & jnp.logical_not(mine))
        def _():
            columns = pl.ds(pl.multiple_of(item * size, size), size)
            remote(
                x_ref.at[:, :, columns], x_in, x_sent.at[other_pair], x_came, tp=to_tp, dp=to_dp
            ).wait_send()

    @pl.loop(low, high_end)
    def _(to_unit):
        for bit in range(2):
            to_section = to_unit * 2 + bit
            for to_core in range(2):

                @pl.when(jnp.logical_not((to_section == section) & (core == to_core)))
                def _():
                    rows = pl.ds(to_core * half, half)
                    remote(
                        stage.at[0],
                        params.at[section],
                        p_sent.at[to_section, to_core],
                        p_came.at[section],
                        tp=sibling,
                    ).wait_send()
                    remote(
                        mix_ref.at[0, rows],
                        weights.at[section, rows],
                        w_sent.at[to_section, to_core],
                        w_came.at[section],
                        tp=sibling,
                    ).wait_send()

    @pl.when(active)
    def _():
        @pl.loop(0, layers)
        def _(layer):
            forward_half(layer).wait_send()
            exchange1(layer).wait_send()
            exchange2(layer).wait_send()
            exchange3(layer).wait_send()

            @pl.when(jnp.logical_not(is_owner(layer)))
            def _():
                to_owner(layer).wait_send()


def shards(inputs, norm_gain, norm_bias, mix):
    sections, tps, replicas = (lax.axis_size(name) for name in ("section", "tp", "dp"))
    batches, block, features = inputs.shape
    heads, size = mix.shape[1], mix.shape[2]
    rows = batches * block
    param_count = sections * tps * (2 * features + heads * size * size)
    loss_scale = 1.0 / math.sqrt(rows * replicas)
    piece = size // 8 + 8
    f32, bf16 = jnp.float32, jnp.bfloat16
    dma = pltpu.SemaphoreType.DMA
    flops = 3 * 2 * sections * rows * size * size
    raw, scale = pl.pallas_call(
        functools.partial(relay_kernel, loss_scale, float(param_count)),
        out_shape=(
            jax.ShapeDtypeStruct((heads, piece, size), f32),
            jax.ShapeDtypeStruct((1, size), f32),
        ),
        in_specs=[
            pl.BlockSpec(memory_space=pl.ANY),
            pl.BlockSpec(memory_space=pltpu.VMEM),
            pl.BlockSpec(memory_space=pltpu.VMEM),
            pl.BlockSpec(memory_space=pl.ANY),
        ],
        out_specs=[pl.BlockSpec(memory_space=pltpu.VMEM)] * 2,
        scratch_shapes=[
            pltpu.VMEM((batches, block, size), bf16),
            pltpu.VMEM((heads, 2, size), f32),
            pltpu.VMEM((sections, 2, size), f32),
            pltpu.VMEM((sections, size, size), bf16),
            pltpu.VMEM((rows, size), bf16),
            pltpu.VMEM((sections, rows, size), f32),
            pltpu.VMEM((sections, rows, size), f32),
            pltpu.VMEM((sections, rows, size), bf16),
            pltpu.VMEM((sections, rows, size), f32),
            pltpu.VMEM((sections, size, size), f32),
            pltpu.VMEM((sections, 8, size), f32),
            pltpu.VMEM((sections, size // 2 + 8, size), f32),
            pltpu.VMEM((sections, size // 4 + 8, size), f32),
            pltpu.VMEM((sections, piece, size), f32),
            pltpu.VMEM((sections, piece, size), f32),
            pltpu.VMEM((sections, size // 2 + 8, size), f32),
            pltpu.VMEM((sections, size // 4 + 8, size), f32),
            pltpu.VMEM((sections, piece, size), f32),
            pltpu.VMEM((heads, piece, size), f32),
            pltpu.VMEM((4, 1, size), f32),
            pltpu.VMEM((replicas, 1, size), f32),
            pltpu.VMEM((sections, 1, size), f32),
            pltpu.VMEM((tps, 1, size), f32),
            dma((replicas // 2,)),
            dma,
            dma((sections, 2)),
            dma((sections,)),
            dma((sections, 2)),
            dma((sections,)),
            dma((sections,)),
            dma((sections,)),
            dma((sections,)),
            dma((sections,)),
            dma((sections,)),
            dma((sections,)),
            dma((sections,)),
            dma((sections,)),
            dma((sections,)),
            dma((heads,)),
            dma((replicas,)),
            dma((replicas,)),
            dma((sections,)),
            dma((sections,)),
            dma((tps,)),
            dma((tps,)),
        ],
        compiler_params=pltpu.CompilerParams(
            vmem_limit_bytes=40 << 20, has_side_effects=True
        ),
        cost_estimate=pl.CostEstimate(
            flops=flops, bytes_accessed=4 << 20, transcendentals=sections * rows * size
        ),
        name="relay",
    )(inputs, norm_gain, norm_bias, mix[0])
    raw = raw * scale[None]
    return (
        raw[:, size // 8].reshape(1, features),
        raw[:, size // 8 + 1].reshape(1, features),
        raw[None, :, : size // 8],
    )


def solution(mesh):
    placed = (
        P(None, "dp", "tp"),
        P("section", "tp"),
        P("section", "tp"),
        P("section", "tp", None, None),
    )
    return jax.shard_map(
        shards,
        mesh=mesh,
        in_specs=placed,
        out_specs=(P("section", "tp"), P("section", "tp"), P("section", "tp", "dp", None)),
        check_vma=False,
    )
```

time: 218 us -> 83.4 us (0.38)
  blocking collectives: 133 us -> 0 us
  Pallas kernels: 11.1 us -> 77.7 us
  waiting for transfers between devices: 30.5 us -> 0 us
  starting transfers between devices: 21 us -> 0 us
  between operations: 16.1 us -> 0.66 us
  other arithmetic: 3.3 us -> 0.02 us
  local copies, waits for them, and re-layouts: 2.49 us -> 4.76 us
    psum x2 -> x0, blocking collectives: 123 us -> none  [the longest x1 99.2 us: shards(): total = lax.psum(squares, ('section', 'tp', 'dp'))]
    pallas_call x1, Pallas kernels: 11.1 us -> 77.7 us  [shards(): pl.pallas_call(functools.partial(relay_kernel, loss_scale, float(param_co...]
    all_to_all x3 -> x0, waiting for transfers between devices: 26.3 us -> none  [the longest x1 15.4 us: shards(): weights = lax.all_to_all(weights, 'section', 0, 0, tiled=True)]
    all_to_all x3 -> x0, starting transfers between devices: 20.9 us -> none  [the longest x1 10.4 us: shards(): params = lax.all_to_all(params, 'section', 0, 0, tiled=True)]
    all_to_all x1 -> x0, blocking collectives: 9.98 us -> none  [shards(): vec_sum = lax.all_to_all(vec_sum, 'section', 0, 0, tiled=True)[:heads]]
    reduce_scatter x1 -> x0, waiting for transfers between devices: 4.2 us -> none  [shards(): mix_sum = lax.psum_scatter(mix_part, 'dp', scatter_dimension=1, tiled=True)]
    unnamed x2 -> x8, local copies, waits for them, and re-layouts: 0.01 us -> 3.5 us
  transfers between devices with their start and end apart: 4 -> 0, of which waited for: 4 -> 0; matrix products, arithmetic and copies ran while one was open for 1% -> 0% of each run, Pallas kernels for 0% -> 0%
where the time goes in v2:
time: 83.4 us; the launch traced here: 83.1 us
  Pallas kernels  77.7 us (93%)
  local copies, waits for them, and re-layouts  4.76 us (6%)
    pallas_call x1, Pallas kernels, shards(): pl.pallas_call(functools.partial(relay_kernel, loss_scale, float(param_co...  77.7 us
    unnamed x8, local copies, waits for them, and re-layouts  3.5 us

profile of v2, /device:TPU:1, one launch (start us, length us, event | category | flops | bytes accessed | tf_op | source)
XLA Modules:
  0.0 83.1 jit_solution(6141967433042811839)
XLA Ops:
  0.6 0.0 copy-start
  0.6 1.1 %copy-done = bf16[4,48,1792]{2,1,0:T(8,128)(2,1)S(1)} copy-done((bf16[4,48,1792]{2,1,0:T(8,128)(2,1)S(1)}, bf16[4,48,1792]{2,1,0:T(8,128)(2,1)}, u32[]{:S(2)}) %copy-start) | copy-done | bytes 688152
  1.7 0.0 copy-start.1
  1.7 1.0 %copy-done.1 = bf16[1,14,128,128]{3,2,1,0:T(8,128)(2,1)S(1)} copy-done((bf16[1,14,128,128]{3,2,1,0:T(8,128)(2,1)S(1)}, bf16[1,14,128,128]{3,2,1,0:T(8,128)(2,1)}, u32[]{:S(2)}) %copy-start.1) | copy-done | bytes 458776
  2.8 0.0 copy-start.2
  2.8 0.7 copy-done.2
  3.4 0.0 copy-start.3
  3.4 0.7 copy-done.3
  4.1 77.7 %relay.1 = (f32[14,24,128]{2,1,0:T(8,128)S(1)}, f32[1,128]{1,0:T(1,128)S(1)}) custom-call(bf16[4,48,1792]{2,1,0:T(8,128)(2,1)S(1)} %copy-done, f32[1,1792]{1,0:T(1,128)S(1)} %copy-done.2, f32[1,1792]{1,0:T(1,128)S(1)} %copy-done.3, bf16[14,128,128]{2,1,0:T(8,128)(2,1)S(1)} %bitcast.8), custom_call_target="tpu_custom_call" | custom-call | flops 301989888 | bytes 4194304 | tf_op jit(solution)/shard_map/relay/pallas_call | solution.py:476
  81.9 0.6 slice_bitcast_fusion.1
  82.5 0.7 slice_bitcast_fusion
  (1 shorter events, 0.0 us)
Async XLA Ops:
  0.6 1.1 %copy-start = (bf16[4,48,1792]{2,1,0:T(8,128)(2,1)S(1)}, bf16[4,48,1792]{2,1,0:T(8,128)(2,1)}, u32[]{:S(2)}) copy-start(bf16[4,48,1792]{2,1,0:T(8,128)(2,1)} %x_ref.1) | copy-start | bytes 2064388
  1.7 1.0 %copy-start.1 = (bf16[1,14,128,128]{3,2,1,0:T(8,128)(2,1)S(1)}, bf16[1,14,128,128]{3,2,1,0:T(8,128)(2,1)}, u32[]{:S(2)}) copy-start(bf16[1,14,128,128]{3,2,1,0:T(8,128)(2,1)} %param.7) | copy-start | bytes 1376260
  2.8 0.7 copy-start.2
  3.4 0.7 copy-start.3

commit v3 on v2

--- a/solution.py
+++ b/solution.py
@@ -49,7 +49,8 @@
 
 
 MESH = pl.DeviceIdType.MESH
-LAG = 3
+LAG_CORE = 3
+LAG_CHIP = 8
 AHEAD = 2
 
 
@@ -63,6 +64,7 @@
     raw_ref,
     scale_ref,
     x_in,
+    rows_in,
     stage,
     params,
     weights,
@@ -75,16 +77,14 @@
     part_vec,
     out1,
     out2,
-    out3,
     out4,
     in1,
     in2,
-    in3,
     in4,
     square,
-    all_dp,
-    all_section,
-    all_tp,
+    all_column,
+    all_plane,
+    rows_came,
     x_sent,
     x_came,
     w_sent,
@@ -95,18 +95,14 @@
     f_came,
     sent1,
     sent2,
-    sent3,
     sent4,
     came1,
     came2,
-    came3,
     came4,
-    dp_sent,
-    dp_came,
-    section_sent,
-    section_came,
-    tp_sent,
-    tp_came,
+    column_sent,
+    column_came,
+    plane_sent,
+    plane_came,
 ):
     section, tp, dp = (lax.axis_index(name) for name in ("section", "tp", "dp"))
     layers = weights.shape[0]
@@ -143,6 +139,42 @@
         def _():
             remote(source, target, sent, came, **where).start()
 
+    for index, ref in enumerate((gain_ref, bias_ref)):
+        pltpu.make_async_copy(ref, rows_in.at[index], rows_came.at[index]).start()
+    sections, dps = lax.axis_size("section"), lax.axis_size("dp")
+    column, x_place = lax.rem(section, 4), lax.div(section, 4)
+    barrier = pltpu.get_barrier_semaphore()
+
+    def greet(**where):
+        pl.semaphore_signal(barrier, inc=1, device_id=where, device_id_type=MESH)
+
+    greeted = 0
+    for x_step in range(1, sections // 4):
+        for step in range(1, dps):
+            greet(
+                section=lax.rem(x_place + x_step, sections // 4) * 4 + column,
+                dp=lax.rem(dp + step, dps),
+            )
+            greeted += 1
+    for step in range(4):
+        for to_core in range(2):
+            greet(section=x_place * 4 + step, tp=(1 - high) * 2 + to_core)
+            greeted += 1
+    for step in range(1, sections):
+        for to_core in range(2):
+            greet(section=lax.rem(section + step, sections), tp=high * 2 + to_core)
+            greeted += 1
+    for step in range(1, dps):
+        for to_core in range(2):
+            greet(dp=lax.rem(dp + step, dps), tp=high * 2 + to_core)
+            greeted += 1
+    greet(section=unit * 2 + 1 - z_bit, dp=pair * 2 + 1 - y_bit)
+    greet(tp=high * 2 + 1 - core)
+    greeted += 2
+    part_vec[...] = jnp.zeros_like(part_vec)
+    square[...] = jnp.zeros_like(square)
+    pl.semaphore_wait(barrier, greeted)
+
     def x_plan(other_pair):
         here = unit * pairs + other_pair
         goes = (lax.div(here, heads) == core) & (y_bit == z_bit)
@@ -167,12 +199,11 @@
                 dp=to_dp,
             )
 
-    for item in range(heads):
-        columns = slice(item * size, (item + 1) * size)
-        stage[item, 0:1] = gain_ref[0:1, columns]
-        stage[item, 1:2] = bias_ref[0:1, columns]
-    part_vec[...] = jnp.zeros_like(part_vec)
-    square[...] = jnp.zeros_like(square)
+    for index, ref in enumerate((gain_ref, bias_ref)):
+        pltpu.make_async_copy(ref, rows_in.at[index], rows_came.at[index]).wait()
+        for item in range(heads):
+            columns = slice(item * size, (item + 1) * size)
+            stage[item, index : index + 1] = rows_in[index, 0:1, columns]
     middle = lax.div(heads + pairs - 1 - pair, pairs)
     stop = lax.div(2 * heads + pairs - 1 - pair, pairs)
     low = jnp.where(core == 0, 0, middle)
@@ -224,22 +255,18 @@
             out1.at[layer], in1.at[layer], sent1.at[layer], came1.at[layer], tp=sibling
         )
 
-    def exchange2(layer):
+    chip = y_bit * 2 + z_bit
+
+    def exchange2(layer, flip):
+        to_y = lax.rem(y_bit + flip // 2, 2)
+        to_z = lax.rem(z_bit + flip % 2, 2)
         return remote(
-            out2.at[layer],
-            in2.at[layer],
-            sent2.at[layer],
-            came2.at[layer],
-            dp=pair * 2 + 1 - y_bit,
-        )
-
-    def exchange3(layer):
-        return remote(
-            out3.at[layer],
-            in3.at[layer],
-            sent3.at[layer],
-            came3.at[layer],
-            section=unit * 2 + 1 - z_bit,
+            out2.at[layer, to_y * 2 + to_z],
+            in2.at[layer, chip],
+            sent2.at[layer, flip - 1],
+            came2.at[layer, flip - 1],
+            section=unit * 2 + to_z,
+            dp=pair * 2 + to_y,
         )
 
     def to_owner(layer):
@@ -289,7 +316,7 @@
 
         flow[...] = (flow[...].astype(jnp.float32) * loss_scale).astype(jnp.bfloat16)
 
-        @pl.loop(0, layers + 3 * LAG)
+        @pl.loop(0, layers + LAG_CORE + LAG_CHIP)
         def _(tick):
             @pl.when(tick < layers)
             def _():
@@ -311,53 +338,31 @@
                 out1[layer, half:] = part_vec[layer]
                 exchange1(layer).start()
 
-            step2 = tick - LAG
+            step2 = tick - LAG_CORE
 
             @pl.when((step2 >= 0) & (step2 < layers))
             def _():
                 layer = layers - 1 - step2
                 exchange1(layer).wait_recv()
-                away = (1 - y_bit) * quarter
-                out2[layer, 0:quarter] = rows_of(
-                    part_mix, layer, core * half + away, quarter
-                ) + rows_of(in1, layer, away, quarter)
-                out2[layer, quarter:] = part_vec[layer] + in1[layer, half:]
-                exchange2(layer).start()
-
-            step3 = tick - 2 * LAG
+                mix_half = rows_of(part_mix, layer, core * half, half) + in1[layer, 0:half]
+                vec_half = part_vec[layer] + in1[layer, half:]
+                for index in range(4):
+                    out2[layer, index, 0:eighth] = mix_half[index * eighth : (index + 1) * eighth]
+                    out2[layer, index, eighth:] = vec_half
+                for flip in (3, 2, 1):
+                    exchange2(layer, flip).start()
+                in2[layer, chip] = out2[layer, chip]
+
+            step3 = tick - LAG_CORE - LAG_CHIP
 
             @pl.when((step3 >= 0) & (step3 < layers))
             def _():
                 layer = layers - 1 - step3
-                exchange2(layer).wait_recv()
-                away = (1 - z_bit) * eighth
-                out3[layer, 0:eighth] = (
-                    rows_of(part_mix, layer, core * half + y_bit * quarter + away, eighth)
-                    + rows_of(in1, layer, y_bit * quarter + away, eighth)
-                ) + rows_of(in2, layer, away, eighth)
-                out3[layer, eighth:] = (part_vec[layer] + in1[layer, half:]) + in2[
-                    layer, quarter:
-                ]
-                exchange3(layer).start()
-
-            step4 = tick - 3 * LAG
-
-            @pl.when((step4 >= 0) & (step4 < layers))
-            def _():
-                layer = layers - 1 - step4
-                exchange3(layer).wait_recv()
-                mix_sum = (
-                    (
-                        rows_of(part_mix, layer, part * eighth, eighth)
-                        + rows_of(in1, layer, y_bit * quarter + z_bit * eighth, eighth)
-                    )
-                    + rows_of(in2, layer, z_bit * eighth, eighth)
-                ) + in3[layer, 0:eighth]
-                vec_sum = (
-                    (part_vec[layer] + in1[layer, half:]) + in2[layer, quarter:]
-                ) + in3[layer, eighth:]
-                out4[layer, 0:eighth] = mix_sum
-                out4[layer, eighth:] = vec_sum
+                for flip in (1, 2, 3):
+                    exchange2(layer, flip).wait_recv()
+                whole = (in2[layer, 0] + in2[layer, 1]) + (in2[layer, 2] + in2[layer, 3])
+                mix_sum, vec_sum = whole[:eighth], whole[eighth:]
+                out4[layer] = whole
 
                 @pl.when(is_owner(layer))
                 def _():
@@ -371,41 +376,41 @@
                     1.0 / lax.axis_size("dp")
                 ) * jnp.sum(vec_sum * vec_sum, axis=0, keepdims=True)
 
+    def column_place(step):
+        to_column = lax.rem(column + lax.div(step, 4), 4)
+        to_tp = lax.rem(tp + lax.rem(step, 4), 4)
+        return to_column * 4 + to_tp, dict(section=x_place * 4 + to_column, tp=to_tp)
+
+    def plane_place(step):
+        to_x = lax.rem(x_place + lax.div(step, dps), sections // 4)
+        to_dp = lax.rem(dp + lax.rem(step, dps), dps)
+        return to_x * dps + to_dp, dict(section=to_x * 4 + column, dp=to_dp)
+
     stages = (
-        ("dp", dp, all_dp, dp_sent, dp_came),
-        ("section", section, all_section, section_sent, section_came),
-        ("tp", tp, all_tp, tp_sent, tp_came),
+        (column_place, all_column, column_sent, column_came),
+        (plane_place, all_plane, plane_sent, plane_came),
     )
-    for index, (name, me, slots, sent, came) in enumerate(stages):
-        count = lax.axis_size(name)
-
-        def copy_to(peer, index=index, name=name, me=me, slots=slots, sent=sent, came=came):
-            return remote(
-                square.at[index], slots.at[me], sent.at[peer], came.at[me], **{name: peer}
-            )
-
-        def copy_from(peer, index=index, name=name, slots=slots, sent=sent, came=came):
-            return remote(
-                square.at[index], slots.at[peer], sent.at[peer], came.at[peer], **{name: peer}
-            )
-
-        slots[me] = square[index]
-
-        @pl.loop(1, count)
-        def _(step):
-            copy_to(lax.rem(me + step, count)).start()
-
-        @pl.loop(1, count)
-        def _(step):
-            copy_from(lax.rem(me + step, count)).wait_recv()
-
+    for index, (place_of, slots, sent, came) in enumerate(stages):
+        count = slots.shape[0]
+        mine, _ = place_of(0)
+        slots[mine] = square[index]
+
+        def copy_to(step, index=index, place_of=place_of, slots=slots, sent=sent, came=came):
+            place, where = place_of(step)
+            here, _ = place_of(0)
+            return remote(square.at[index], slots.at[here], sent.at[place], came.at[here], **where)
+
+        def copy_from(step, index=index, place_of=place_of, slots=slots, sent=sent, came=came):
+            place, where = place_of(step)
+            return remote(square.at[index], slots.at[place], sent.at[place], came.at[place], **where)
+
+        for step in range(1, count):
+            copy_to(step).start()
+        for step in range(1, count):
+            copy_from(step).wait_recv()
         square[index + 1] = jnp.sum(slots[...], axis=0)
 
-        @pl.loop(1, count)
-        def _(step):
-            copy_to(lax.rem(me + step, count)).wait_send()
-
-    total = jnp.sum(square[3], axis=-1, keepdims=True)
+    total = jnp.sum(square[2], axis=-1, keepdims=True)
     scale_ref[...] = jnp.broadcast_to(lax.rsqrt(total / param_count + GRAD_EPS), scale_ref.shape)
 
     @pl.loop(0, heads)
@@ -413,6 +418,15 @@
         remote(out4.at[0], in4.at[item], sent4.at[0], came4.at[item], tp=sibling).wait_recv()
 
     raw_ref[...] = in4[...]
+
+    for index, (place_of, slots, sent, came) in enumerate(stages):
+
+        @pl.loop(1, slots.shape[0])
+        def _(step, index=index, place_of=place_of, slots=slots, sent=sent, came=came):
+            place, where = place_of(step)
+            remote(
+                square.at[index], slots.at[place], sent.at[place], came.at[place], **where
+            ).wait_send()
 
     for other_pair in range(pairs):
         item, goes, mine, to_dp, to_tp = x_plan(other_pair)
@@ -454,8 +468,8 @@
         def _(layer):
             forward_half(layer).wait_send()
             exchange1(layer).wait_send()
-            exchange2(layer).wait_send()
-            exchange3(layer).wait_send()
+            for flip in (1, 2, 3):
+                exchange2(layer, flip).wait_send()
 
             @pl.when(jnp.logical_not(is_owner(layer)))
             def _():
@@ -481,13 +495,14 @@
         ),
         in_specs=[
             pl.BlockSpec(memory_space=pl.ANY),
-            pl.BlockSpec(memory_space=pltpu.VMEM),
-            pl.BlockSpec(memory_space=pltpu.VMEM),
+            pl.BlockSpec(memory_space=pl.ANY),
+            pl.BlockSpec(memory_space=pl.ANY),
             pl.BlockSpec(memory_space=pl.ANY),
         ],
         out_specs=[pl.BlockSpec(memory_space=pltpu.VMEM)] * 2,
         scratch_shapes=[
             pltpu.VMEM((batches, block, size), bf16),
+            pltpu.VMEM((2, 1, features), f32),
             pltpu.VMEM((heads, 2, size), f32),
             pltpu.VMEM((sections, 2, size), f32),
             pltpu.VMEM((sections, size, size), bf16),
@@ -499,17 +514,15 @@
             pltpu.VMEM((sections, size, size), f32),
             pltpu.VMEM((sections, 8, size), f32),
             pltpu.VMEM((sections, size // 2 + 8, size), f32),
-            pltpu.VMEM((sections, size // 4 + 8, size), f32),
-            pltpu.VMEM((sections, piece, size), f32),
+            pltpu.VMEM((sections, 4, piece, size), f32),
             pltpu.VMEM((sections, piece, size), f32),
             pltpu.VMEM((sections, size // 2 + 8, size), f32),
-            pltpu.VMEM((sections, size // 4 + 8, size), f32),
-            pltpu.VMEM((sections, piece, size), f32),
+            pltpu.VMEM((sections, 4, piece, size), f32),
             pltpu.VMEM((heads, piece, size), f32),
-            pltpu.VMEM((4, 1, size), f32),
-            pltpu.VMEM((replicas, 1, size), f32),
-            pltpu.VMEM((sections, 1, size), f32),
-            pltpu.VMEM((tps, 1, size), f32),
+            pltpu.VMEM((3, 1, size), f32),
+            pltpu.VMEM((4 * tps, 1, size), f32),
+            pltpu.VMEM((sections // 4 * replicas, 1, size), f32),
+            dma((2,)),
             dma((replicas // 2,)),
             dma,
             dma((sections, 2)),
@@ -519,22 +532,18 @@
             dma((sections,)),
             dma((sections,)),
             dma((sections,)),
-            dma((sections,)),
-            dma((sections,)),
-            dma((sections,)),
-            dma((sections,)),
-            dma((sections,)),
-            dma((sections,)),
+            dma((sections, 3)),
+            dma((sections,)),
+            dma((sections,)),
+            dma((sections, 3)),
             dma((heads,)),
-            dma((replicas,)),
-            dma((replicas,)),
-            dma((sections,)),
-            dma((sections,)),
-            dma((tps,)),
-            dma((tps,)),
+            dma((4 * tps,)),
+            dma((4 * tps,)),
+            dma((sections // 4 * replicas,)),
+            dma((sections // 4 * replicas,)),
         ],
         compiler_params=pltpu.CompilerParams(
-            vmem_limit_bytes=40 << 20, has_side_effects=True
+            vmem_limit_bytes=60 << 20, collective_id=0, has_side_effects=True
         ),
         cost_estimate=pl.CostEstimate(
             flops=flops, bytes_accessed=4 << 20, transcendentals=sections * rows * size

time: 83.4 us -> 66.9 us (0.80)
  Pallas kernels: 77.7 us -> 63.2 us
  local copies, waits for them, and re-layouts: 4.76 us -> 1.86 us
  other arithmetic: 0.02 us -> 0.93 us
    pallas_call x1, Pallas kernels: 77.7 us -> 63.2 us  [shards(): pl.pallas_call(functools.partial(relay_kernel, loss_scale, float(param_co...]
    unnamed x8 -> x2, local copies, waits for them, and re-layouts: 3.5 us -> 0.6 us
    mul x1, other arithmetic: 0.02 us -> 0.93 us  [shards(): raw = raw * scale[None]]
where the time goes in v3:
time: 66.9 us; the launch traced here: 66.6 us
  Pallas kernels  63.2 us (94%)
  local copies, waits for them, and re-layouts  1.86 us (3%)
  other arithmetic  0.93 us (1%)
    pallas_call x1, Pallas kernels, shards(): pl.pallas_call(functools.partial(relay_kernel, loss_scale, float(param_co...  63.2 us

profile of v3, /device:TPU:1, one launch (start us, length us, event | category | flops | bytes accessed | tf_op | source)
XLA Modules:
  0.0 66.6 jit_solution(11960105996181392346)
XLA Ops:
  0.6 63.2 %relay.1 = (f32[14,24,128]{2,1,0:T(8,128)}, f32[1,128]{1,0:T(1,128)}) custom-call(bf16[4,48,1792]{2,1,0:T(8,128)(2,1)} %x_ref.1, f32[1,1792]{1,0:T(1,128)} %gain_ref.1, f32[1,1792]{1,0:T(1,128)} %bias_ref.1, bf16[14,128,128]{2,1,0:T(8,128)(2,1)} %bitcast.8), custom_call_target="tpu_custom_call" | custom-call | flops 301989888 | bytes 4194304 | tf_op jit(solution)/shard_map/relay/pallas_call | solution.py:490
  63.8 0.0 copy-start
  63.9 0.6 copy-done
  64.5 0.9 %broadcast_multiply_fusion = f32[14,24,128]{2,1,0:T(8,128)S(1)} fusion(f32[14,24,128]{2,1,0:T(8,128)} %get-tuple-element.5, f32[128]{0:T(128)S(1)} %bitcast.9), kind=kLoop, calls=%fused_computation.1 | loop fusion | flops 43008 | bytes 344576 | tf_op jit(solution)/shard_map/mul | solution.py:553
  65.4 0.6 slice_bitcast_fusion.1
  66.0 0.7 slice_bitcast_fusion
Async XLA Ops:
  63.8 0.6 copy-start

commit v4 on v3

--- a/solution.py
+++ b/solution.py
@@ -51,7 +51,7 @@
 MESH = pl.DeviceIdType.MESH
 LAG_CORE = 3
 LAG_CHIP = 8
-AHEAD = 2
+AHEAD = 5
 
 
 def relay_kernel(
@@ -61,8 +61,7 @@
     gain_ref,
     bias_ref,
     mix_ref,
-    raw_ref,
-    scale_ref,
+    grads_ref,
     x_in,
     rows_in,
     stage,
@@ -108,7 +107,8 @@
     layers = weights.shape[0]
     heads = mix_ref.shape[0]
     size = mix_ref.shape[1]
-    half, quarter, eighth = size // 2, size // 4, size // 8
+    half, eighth = size // 2, size // 8
+    half_long, long = half + 2, eighth + 2
     pairs = lax.axis_size("dp") // 2
     core, high = lax.rem(tp, 2), lax.div(tp, 2)
     unit, z_bit = lax.div(section, 2), lax.rem(section, 2)
@@ -171,7 +171,6 @@
     greet(section=unit * 2 + 1 - z_bit, dp=pair * 2 + 1 - y_bit)
     greet(tp=high * 2 + 1 - core)
     greeted += 2
-    part_vec[...] = jnp.zeros_like(part_vec)
     square[...] = jnp.zeros_like(square)
     pl.semaphore_wait(barrier, greeted)
 
@@ -252,7 +251,7 @@
 
     def exchange1(layer):
         return remote(
-            out1.at[layer], in1.at[layer], sent1.at[layer], came1.at[layer], tp=sibling
+            out1.at[layer, 0:half_long], in1.at[layer, 0:half_long], sent1.at[layer], came1.at[layer], tp=sibling
         )
 
     chip = y_bit * 2 + z_bit
@@ -261,8 +260,8 @@
         to_y = lax.rem(y_bit + flip // 2, 2)
         to_z = lax.rem(z_bit + flip % 2, 2)
         return remote(
-            out2.at[layer, to_y * 2 + to_z],
-            in2.at[layer, chip],
+            out2.at[layer, to_y * 2 + to_z, 0:long],
+            in2.at[layer, chip, 0:long],
             sent2.at[layer, flip - 1],
             came2.at[layer, flip - 1],
             section=unit * 2 + to_z,
@@ -271,8 +270,8 @@
 
     def to_owner(layer):
         return remote(
-            out4.at[layer],
-            in4.at[head],
+            out4.at[layer, 0:long],
+            in4.at[head, 0:long],
             sent4.at[layer],
             came4.at[head],
             section=layer,
@@ -335,7 +334,7 @@
                 part_vec[layer, 0:1] = gain_part
                 part_vec[layer, 1:2] = bias_part
                 out1[layer, 0:half] = rows_of(part_mix, layer, (1 - core) * half, half)
-                out1[layer, half:] = part_vec[layer]
+                out1[layer, half:half_long] = part_vec[layer]
                 exchange1(layer).start()
 
             step2 = tick - LAG_CORE
@@ -345,13 +344,13 @@
                 layer = layers - 1 - step2
                 exchange1(layer).wait_recv()
                 mix_half = rows_of(part_mix, layer, core * half, half) + in1[layer, 0:half]
-                vec_half = part_vec[layer] + in1[layer, half:]
+                vec_half = part_vec[layer] + in1[layer, half:half_long]
                 for index in range(4):
                     out2[layer, index, 0:eighth] = mix_half[index * eighth : (index + 1) * eighth]
-                    out2[layer, index, eighth:] = vec_half
+                    out2[layer, index, eighth:long] = vec_half
                 for flip in (3, 2, 1):
                     exchange2(layer, flip).start()
-                in2[layer, chip] = out2[layer, chip]
+                in2[layer, chip, 0:long] = out2[layer, chip, 0:long]
 
             step3 = tick - LAG_CORE - LAG_CHIP
 
@@ -360,13 +359,19 @@
                 layer = layers - 1 - step3
                 for flip in (1, 2, 3):
                     exchange2(layer, flip).wait_recv()
-                whole = (in2[layer, 0] + in2[layer, 1]) + (in2[layer, 2] + in2[layer, 3])
-                mix_sum, vec_sum = whole[:eighth], whole[eighth:]
-                out4[layer] = whole
+                mix_sum, vec_sum = (
+                    (in2[layer, 0, rows] + in2[layer, 1, rows])
+                    + (in2[layer, 2, rows] + in2[layer, 3, rows])
+                    for rows in (slice(0, eighth), slice(eighth, long))
+                )
+                out4[layer, 0:eighth] = mix_sum
+                out4[layer, eighth:long] = vec_sum
 
                 @pl.when(is_owner(layer))
                 def _():
-                    pltpu.make_async_copy(out4.at[layer], in4.at[head], came4.at[head]).start()
+                    pltpu.make_async_copy(
+                        out4.at[layer, 0:long], in4.at[head, 0:long], came4.at[head]
+                    ).start()
 
                 @pl.when(jnp.logical_not(is_owner(layer)))
                 def _():
@@ -411,13 +416,13 @@
         square[index + 1] = jnp.sum(slots[...], axis=0)
 
     total = jnp.sum(square[2], axis=-1, keepdims=True)
-    scale_ref[...] = jnp.broadcast_to(lax.rsqrt(total / param_count + GRAD_EPS), scale_ref.shape)
-
-    @pl.loop(0, heads)
-    def _(item):
-        remote(out4.at[0], in4.at[item], sent4.at[0], came4.at[item], tp=sibling).wait_recv()
-
-    raw_ref[...] = in4[...]
+    scale = lax.rsqrt(total / param_count + GRAD_EPS)
+
+    for item in range(heads):
+        remote(
+            out4.at[0, 0:long], in4.at[item, 0:long], sent4.at[0], came4.at[item], tp=sibling
+        ).wait_recv()
+        grads_ref[item, 0:long] = in4[item, 0:long] * scale
 
     for index, (place_of, slots, sent, came) in enumerate(stages):
 
@@ -487,19 +492,16 @@
     f32, bf16 = jnp.float32, jnp.bfloat16
     dma = pltpu.SemaphoreType.DMA
     flops = 3 * 2 * sections * rows * size * size
-    raw, scale = pl.pallas_call(
+    grads = pl.pallas_call(
         functools.partial(relay_kernel, loss_scale, float(param_count)),
-        out_shape=(
-            jax.ShapeDtypeStruct((heads, piece, size), f32),
-            jax.ShapeDtypeStruct((1, size), f32),
-        ),
+        out_shape=jax.ShapeDtypeStruct((heads, piece, size), f32),
         in_specs=[
             pl.BlockSpec(memory_space=pl.ANY),
             pl.BlockSpec(memory_space=pl.ANY),
             pl.BlockSpec(memory_space=pl.ANY),
             pl.BlockSpec(memory_space=pl.ANY),
         ],
-        out_specs=[pl.BlockSpec(memory_space=pltpu.VMEM)] * 2,
+        out_specs=pl.BlockSpec(memory_space=pltpu.VMEM),
         scratch_shapes=[
             pltpu.VMEM((batches, block, size), bf16),
             pltpu.VMEM((2, 1, features), f32),
@@ -512,7 +514,7 @@
             pltpu.VMEM((sections, rows, size), bf16),
             pltpu.VMEM((sections, rows, size), f32),
             pltpu.VMEM((sections, size, size), f32),
-            pltpu.VMEM((sections, 8, size), f32),
+            pltpu.VMEM((sections, 2, size), f32),
             pltpu.VMEM((sections, size // 2 + 8, size), f32),
             pltpu.VMEM((sections, 4, piece, size), f32),
             pltpu.VMEM((sections, piece, size), f32),
@@ -550,11 +552,10 @@
         ),
         name="relay",
     )(inputs, norm_gain, norm_bias, mix[0])
-    raw = raw * scale[None]
     return (
-        raw[:, size // 8].reshape(1, features),
-        raw[:, size // 8 + 1].reshape(1, features),
-        raw[None, :, : size // 8],
+        grads[:, size // 8].reshape(1, features),
+        grads[:, size // 8 + 1].reshape(1, features),
+        grads[None, :, : size // 8],
     )
 
 

time: 66.9 us -> 62.7 us (0.937)
  Pallas kernels: 63.2 us -> 58.7 us
  local copies, waits for them, and re-layouts: 1.86 us -> 3.06 us
  other arithmetic: 0.93 us -> 0 us
    pallas_call x1, Pallas kernels: 63.2 us -> 58.7 us  [shards(): pl.pallas_call(functools.partial(relay_kernel, loss_scale, float(param_co...]
    mul x1 -> x0, other arithmetic: 0.93 us -> none  [shards(): raw = raw * scale[None]]
    broadcast_in_dim x1, local copies, waits for them, and re-layouts: 0.65 us -> 1.55 us  [shards(): grads[None, :, :size // 8]]
    another operation x1, local copies, waits for them, and re-layouts: 0.61 us -> 1.5 us  [shards(): grads[:, size // 8 + 1].reshape(1, features)]
where the time goes in v4:
time: 62.7 us; the launch traced here: 62.4 us
  Pallas kernels  58.7 us (94%)
  local copies, waits for them, and re-layouts  3.06 us (5%)
  between operations  0.64 us (1%)
    pallas_call x1, Pallas kernels, shards(): pl.pallas_call(functools.partial(relay_kernel, loss_scale, float(param_co...  58.7 us
    broadcast_in_dim x1, local copies, waits for them, and re-layouts, shards(): grads[None, :, :size // 8]  1.55 us
    another operation x1, local copies, waits for them, and re-layouts, shards(): grads[:, size // 8 + 1].reshape(1, features)  1.5 us

profile of v4, /device:TPU:1, one launch (start us, length us, event | category | flops | bytes accessed | tf_op | source)
XLA Modules:
  0.0 62.4 jit_solution(8932902267664287390)
XLA Ops:
  0.6 58.7 %relay.1 = f32[14,24,128]{2,1,0:T(8,128)} custom-call(bf16[4,48,1792]{2,1,0:T(8,128)(2,1)} %x_ref.1, f32[1,1792]{1,0:T(1,128)} %gain_ref.1, f32[1,1792]{1,0:T(1,128)} %bias_ref.1, bf16[14,128,128]{2,1,0:T(8,128)(2,1)} %bitcast.7), custom_call_target="tpu_custom_call" | custom-call | flops 301989888 | bytes 4194304 | tf_op jit(solution)/shard_map/relay/pallas_call | solution.py:495
  59.4 1.5 %slice_bitcast_fusion.1 = (f32[1,1792]{1,0:T(1,128)}, f32[1,1792]{1,0:T(1,128)}) fusion(f32[14,24,128]{2,1,0:T(8,128)} %relay.1), kind=kLoop, calls=%fused_computation.1 | loop fusion | bytes 28672 | tf_op jit(solution)/shard_map/reshape;squeeze | solution.py:557
  60.9 1.6 %slice_bitcast_fusion = f32[1,14,16,128]{3,2,1,0:T(8,128)} fusion(f32[14,24,128]{2,1,0:T(8,128)} %relay.1), kind=kLoop, calls=%fused_computation | loop fusion | bytes 229376 | tf_op jit(solution)/shard_map/broadcast_in_dim | solution.py:558

commit v5 on v4

--- a/solution.py
+++ b/solution.py
@@ -30,7 +30,7 @@
     return (wide + mixed).astype(jnp.bfloat16), normed, inv_std, act, slope
 
 
-def backward_layer(grad, normed, inv_std, act, slope, gain, weights):
+def backward_layer(grad, normed, inv_std, act, slope, gain, weights, is_first):
     grad_act = lax.dot_general(
         grad, weights, (((1,), (1,)), ((), ())), preferred_element_type=jnp.float32
     )
@@ -39,19 +39,20 @@
     )
     grad_pre = grad_act * slope
     gain_term = grad_pre * normed
+    gain_part = jnp.sum(gain_term, axis=0, keepdims=True)
+    bias_part = jnp.sum(grad_pre, axis=0, keepdims=True)
+    if is_first:
+        return None, mix_part, gain_part, bias_part
     grad_norm = grad_pre * gain
     first = jnp.mean(grad_norm, axis=-1, keepdims=True)
     second = jnp.mean(gain_term * gain, axis=-1, keepdims=True)
     grad_in = grad.astype(jnp.float32) + inv_std * (grad_norm - first - normed * second)
-    gain_part = jnp.sum(gain_term, axis=0, keepdims=True)
-    bias_part = jnp.sum(grad_pre, axis=0, keepdims=True)
     return grad_in.astype(jnp.bfloat16), mix_part, gain_part, bias_part
 
 
 MESH = pl.DeviceIdType.MESH
-LAG_CORE = 3
-LAG_CHIP = 8
-AHEAD = 5
+LAG = 3
+AHEAD = 4
 
 
 def relay_kernel(
@@ -208,8 +209,9 @@
     low = jnp.where(core == 0, 0, middle)
     high_end = jnp.where(core == 0, middle, stop)
 
-    @pl.loop(low, high_end)
-    def _(to_unit):
+    @pl.loop(0, high_end - low)
+    def _(turn):
+        to_unit = low + lax.rem(turn + unit, high_end - low)
         item = to_unit * pairs + pair - core * heads
         for bit in range(2):
             to_section = to_unit * 2 + bit
@@ -282,6 +284,17 @@
     def is_owner(layer):
         return (layer == section) & (owner_tp == tp) & (part == dp)
 
+    def start_to_owner(layer):
+        @pl.when(is_owner(layer))
+        def _():
+            pltpu.make_async_copy(
+                out4.at[layer, 0:long], in4.at[head, 0:long], came4.at[head]
+            ).start()
+
+        @pl.when(jnp.logical_not(is_owner(layer)))
+        def _():
+            to_owner(layer).start()
+
     def rows_of(ref, layer, start, count):
         return ref[layer, pl.ds(pl.multiple_of(start, 8), count)]
 
@@ -315,50 +328,44 @@
 
         flow[...] = (flow[...].astype(jnp.float32) * loss_scale).astype(jnp.bfloat16)
 
-        @pl.loop(0, layers + LAG_CORE + LAG_CHIP)
-        def _(tick):
-            @pl.when(tick < layers)
-            def _():
-                layer = layers - 1 - tick
-                grad_in, mix_part, gain_part, bias_part = backward_layer(
-                    flow[...],
-                    normed_s[layer],
-                    inv_s[layer],
-                    act_s[layer],
-                    slope_s[layer],
-                    params[layer, 0:1],
-                    weights[layer],
-                )
+        def back(layer, is_first=False):
+            grad_in, mix_part, gain_part, bias_part = backward_layer(
+                flow[...],
+                normed_s[layer],
+                inv_s[layer],
+                act_s[layer],
+                slope_s[layer],
+                params[layer, 0:1],
+                weights[layer],
+                is_first,
+            )
+            if not is_first:
                 flow[...] = grad_in
-                part_mix[layer] = mix_part
-                part_vec[layer, 0:1] = gain_part
-                part_vec[layer, 1:2] = bias_part
-                out1[layer, 0:half] = rows_of(part_mix, layer, (1 - core) * half, half)
-                out1[layer, half:half_long] = part_vec[layer]
-                exchange1(layer).start()
-
-            step2 = tick - LAG_CORE
-
-            @pl.when((step2 >= 0) & (step2 < layers))
-            def _():
-                layer = layers - 1 - step2
-                exchange1(layer).wait_recv()
-                mix_half = rows_of(part_mix, layer, core * half, half) + in1[layer, 0:half]
-                vec_half = part_vec[layer] + in1[layer, half:half_long]
-                for index in range(4):
-                    out2[layer, index, 0:eighth] = mix_half[index * eighth : (index + 1) * eighth]
-                    out2[layer, index, eighth:long] = vec_half
-                for flip in (3, 2, 1):
-                    exchange2(layer, flip).start()
-                in2[layer, chip, 0:long] = out2[layer, chip, 0:long]
-
-            step3 = tick - LAG_CORE - LAG_CHIP
-
-            @pl.when((step3 >= 0) & (step3 < layers))
-            def _():
-                layer = layers - 1 - step3
+            part_mix[layer] = mix_part
+            part_vec[layer, 0:1] = gain_part
+            part_vec[layer, 1:2] = bias_part
+            out1[layer, 0:half] = rows_of(part_mix, layer, (1 - core) * half, half)
+            out1[layer, half:half_long] = part_vec[layer]
+
+        def sum_cores(layer):
+            mix_half = rows_of(part_mix, layer, core * half, half) + in1[layer, 0:half]
+            vec_half = part_vec[layer] + in1[layer, half:half_long]
+            for index in range(4):
+                out2[layer, index, 0:eighth] = mix_half[index * eighth : (index + 1) * eighth]
+                out2[layer, index, eighth:long] = vec_half
+
+        def to_chips(layer):
+            for flip in (3, 2, 1):
+                exchange2(layer, flip).start()
+
+        def sum_chips(group):
+            for layer in group:
                 for flip in (1, 2, 3):
                     exchange2(layer, flip).wait_recv()
+            for layer in group:
+                in2[layer, chip, 0:long] = out2[layer, chip, 0:long]
+            squares, vec_squares = 0.0, 0.0
+            for layer in group:
                 mix_sum, vec_sum = (
                     (in2[layer, 0, rows] + in2[layer, 1, rows])
                     + (in2[layer, 2, rows] + in2[layer, 3, rows])
@@ -366,20 +373,39 @@
                 )
                 out4[layer, 0:eighth] = mix_sum
                 out4[layer, eighth:long] = vec_sum
-
-                @pl.when(is_owner(layer))
-                def _():
-                    pltpu.make_async_copy(
-                        out4.at[layer, 0:long], in4.at[head, 0:long], came4.at[head]
-                    ).start()
-
-                @pl.when(jnp.logical_not(is_owner(layer)))
-                def _():
-                    to_owner(layer).start()
-
-                square[0] += jnp.sum(mix_sum * mix_sum, axis=0, keepdims=True) + (
-                    1.0 / lax.axis_size("dp")
-                ) * jnp.sum(vec_sum * vec_sum, axis=0, keepdims=True)
+                squares += mix_sum * mix_sum
+                vec_squares += vec_sum * vec_sum
+            square[0] += jnp.sum(squares, axis=0, keepdims=True) + (
+                1.0 / lax.axis_size("dp")
+            ) * jnp.sum(vec_squares, axis=0, keepdims=True)
+
+        @pl.loop(0, LAG)
+        def _(tick):
+            back(layers - 1 - tick)
+            exchange1(layers - 1 - tick).start()
+
+        @pl.loop(LAG, layers - 1)
+        def _(tick):
+            layer = layers - 1 - tick
+            exchange1(layer + LAG).wait_recv()
+            sum_cores(layer + LAG)
+            back(layer)
+            to_chips(layer + LAG)
+            exchange1(layer).start()
+
+        back(0, True)
+        exchange1(0).start()
+        for layer in range(LAG, 0, -1):
+            exchange1(layer).wait_recv()
+            sum_cores(layer)
+            to_chips(layer)
+        early = list(range(LAG + 3, layers))
+        sum_chips(early[len(early) // 2 :])
+        exchange1(0).wait_recv()
+        sum_cores(0)
+        to_chips(0)
+        sum_chips(early[: len(early) // 2])
+        sum_chips(list(range(LAG + 3)))
 
     def column_place(step):
         to_column = lax.rem(column + lax.div(step, 4), 4)
@@ -411,6 +437,14 @@
 
         for step in range(1, count):
             copy_to(step).start()
+        if index == 0:
+
+            @pl.when(active)
+            def _():
+                @pl.loop(0, layers)
+                def _(layer):
+                    start_to_owner(lax.rem(layer + section, layers))
+
         for step in range(1, count):
             copy_from(step).wait_recv()
         square[index + 1] = jnp.sum(slots[...], axis=0)

time: 62.7 us -> 59.5 us (0.949)
  Pallas kernels: 58.7 us -> 55.5 us
    pallas_call x1, Pallas kernels: 58.7 us -> 55.5 us  [shards(): pl.pallas_call(functools.partial(relay_kernel, loss_scale, float(param_co...]
where the time goes in v5:
time: 59.5 us; the launch traced here: 59.2 us
  Pallas kernels  55.5 us (93%)
  local copies, waits for them, and re-layouts  3.06 us (5%)
  between operations  0.64 us (1%)
    pallas_call x1, Pallas kernels, shards(): pl.pallas_call(functools.partial(relay_kernel, loss_scale, float(param_co...  55.5 us
    broadcast_in_dim x1, local copies, waits for them, and re-layouts, shards(): grads[None, :, :size // 8]  1.55 us
    another operation x1, local copies, waits for them, and re-layouts, shards(): grads[:, size // 8 + 1].reshape(1, features)  1.5 us

profile of v5, /device:TPU:1, one launch (start us, length us, event | category | flops | bytes accessed | tf_op | source)
XLA Modules:
  0.0 59.2 jit_solution(7296934063068287103)
XLA Ops:
  0.6 55.5 %relay.1 = f32[14,24,128]{2,1,0:T(8,128)} custom-call(bf16[4,48,1792]{2,1,0:T(8,128)(2,1)} %x_ref.1, f32[1,1792]{1,0:T(1,128)} %gain_ref.1, f32[1,1792]{1,0:T(1,128)} %bias_ref.1, bf16[14,128,128]{2,1,0:T(8,128)(2,1)} %bitcast.7), custom_call_target="tpu_custom_call" | custom-call | flops 301989888 | bytes 4194304 | tf_op jit(solution)/shard_map/relay/pallas_call | solution.py:529
  56.2 1.5 %slice_bitcast_fusion.1 = (f32[1,1792]{1,0:T(1,128)}, f32[1,1792]{1,0:T(1,128)}) fusion(f32[14,24,128]{2,1,0:T(8,128)} %relay.1), kind=kLoop, calls=%fused_computation.1 | loop fusion | bytes 28672 | tf_op jit(solution)/shard_map/reshape;squeeze | solution.py:591
  57.7 1.6 %slice_bitcast_fusion = f32[1,14,16,128]{3,2,1,0:T(8,128)} fusion(f32[14,24,128]{2,1,0:T(8,128)} %relay.1), kind=kLoop, calls=%fused_computation | loop fusion | bytes 229376 | tf_op jit(solution)/shard_map/broadcast_in_dim | solution.py:592

commit v6 on v5

--- a/solution.py
+++ b/solution.py
@@ -51,7 +51,7 @@
 
 
 MESH = pl.DeviceIdType.MESH
-LAG = 3
+LAG = 2
 AHEAD = 4
 
 
@@ -251,21 +251,28 @@
         remote(own, own, w_sent.at[0, 0], w_came.at[layer], tp=sibling).wait_recv()
         forward_half(layer).start()
 
-    def exchange1(layer):
+    def both(couple):
+        return pl.ds(2 * couple, 2)
+
+    def exchange1(couple):
         return remote(
-            out1.at[layer, 0:half_long], in1.at[layer, 0:half_long], sent1.at[layer], came1.at[layer], tp=sibling
+            out1.at[both(couple), 0:half_long],
+            in1.at[both(couple), 0:half_long],
+            sent1.at[couple],
+            came1.at[couple],
+            tp=sibling,
         )
 
     chip = y_bit * 2 + z_bit
 
-    def exchange2(layer, flip):
+    def exchange2(couple, flip):
         to_y = lax.rem(y_bit + flip // 2, 2)
         to_z = lax.rem(z_bit + flip % 2, 2)
         return remote(
-            out2.at[layer, to_y * 2 + to_z, 0:long],
-            in2.at[layer, chip, 0:long],
-            sent2.at[layer, flip - 1],
-            came2.at[layer, flip - 1],
+            out2.at[to_y * 2 + to_z, both(couple), 0:long],
+            in2.at[chip, both(couple), 0:long],
+            sent2.at[couple, flip - 1],
+            came2.at[couple, flip - 1],
             section=unit * 2 + to_z,
             dp=pair * 2 + to_y,
         )
@@ -351,24 +358,30 @@
             mix_half = rows_of(part_mix, layer, core * half, half) + in1[layer, 0:half]
             vec_half = part_vec[layer] + in1[layer, half:half_long]
             for index in range(4):
-                out2[layer, index, 0:eighth] = mix_half[index * eighth : (index + 1) * eighth]
-                out2[layer, index, eighth:long] = vec_half
-
-        def to_chips(layer):
+                out2[index, layer, 0:eighth] = mix_half[index * eighth : (index + 1) * eighth]
+                out2[index, layer, eighth:long] = vec_half
+
+        def sum_pair(couple):
+            exchange1(couple).wait_recv()
+            sum_cores(2 * couple)
+            sum_cores(2 * couple + 1)
+
+        def to_chips(couple):
             for flip in (3, 2, 1):
-                exchange2(layer, flip).start()
-
-        def sum_chips(group):
+                exchange2(couple, flip).start()
+
+        def sum_chips(couples):
+            for couple in couples:
+                for flip in (1, 2, 3):
+                    exchange2(couple, flip).wait_recv()
+            group = [2 * couple + odd for couple in couples for odd in (0, 1)]
             for layer in group:
-                for flip in (1, 2, 3):
-                    exchange2(layer, flip).wait_recv()
-            for layer in group:
-                in2[layer, chip, 0:long] = out2[layer, chip, 0:long]
+                in2[chip, layer, 0:long] = out2[chip, layer, 0:long]
             squares, vec_squares = 0.0, 0.0
             for layer in group:
                 mix_sum, vec_sum = (
-                    (in2[layer, 0, rows] + in2[layer, 1, rows])
-                    + (in2[layer, 2, rows] + in2[layer, 3, rows])
+                    (in2[0, layer, rows] + in2[1, layer, rows])
+                    + (in2[2, layer, rows] + in2[3, layer, rows])
                     for rows in (slice(0, eighth), slice(eighth, long))
                 )
                 out4[layer, 0:eighth] = mix_sum
@@ -379,33 +392,36 @@
                 1.0 / lax.axis_size("dp")
             ) * jnp.sum(vec_squares, axis=0, keepdims=True)
 
+        couples = layers // 2
+
         @pl.loop(0, LAG)
         def _(tick):
-            back(layers - 1 - tick)
-            exchange1(layers - 1 - tick).start()
-
-        @pl.loop(LAG, layers - 1)
+            couple = couples - 1 - tick
+            back(2 * couple + 1)
+            back(2 * couple)
+            exchange1(couple).start()
+
+        @pl.loop(LAG, couples - 1)
         def _(tick):
-            layer = layers - 1 - tick
-            exchange1(layer + LAG).wait_recv()
-            sum_cores(layer + LAG)
-            back(layer)
-            to_chips(layer + LAG)
-            exchange1(layer).start()
-
+            couple = couples - 1 - tick
+            sum_pair(couple + LAG)
+            back(2 * couple + 1)
+            to_chips(couple + LAG)
+            back(2 * couple)
+            exchange1(couple).start()
+
+        back(1)
         back(0, True)
         exchange1(0).start()
-        for layer in range(LAG, 0, -1):
-            exchange1(layer).wait_recv()
-            sum_cores(layer)
-            to_chips(layer)
-        early = list(range(LAG + 3, layers))
-        sum_chips(early[len(early) // 2 :])
-        exchange1(0).wait_recv()
-        sum_cores(0)
+        for couple in range(LAG, 0, -1):
+            sum_pair(couple)
+            to_chips(couple)
+        sum_chips((6, 7))
+        sum_pair(0)
         to_chips(0)
-        sum_chips(early[: len(early) // 2])
-        sum_chips(list(range(LAG + 3)))
+        sum_chips((4, 5))
+        sum_chips((3, 2))
+        sum_chips((1, 0))
 
     def column_place(step):
         to_column = lax.rem(column + lax.div(step, 4), 4)
@@ -506,13 +522,16 @@
         @pl.loop(0, layers)
         def _(layer):
             forward_half(layer).wait_send()
-            exchange1(layer).wait_send()
-            for flip in (1, 2, 3):
-                exchange2(layer, flip).wait_send()
 
             @pl.when(jnp.logical_not(is_owner(layer)))
             def _():
                 to_owner(layer).wait_send()
+
+        @pl.loop(0, layers // 2)
+        def _(couple):
+            exchange1(couple).wait_send()
+            for flip in (1, 2, 3):
+                exchange2(couple, flip).wait_send()
 
 
 def shards(inputs, norm_gain, norm_bias, mix):
@@ -550,10 +569,10 @@
             pltpu.VMEM((sections, size, size), f32),
             pltpu.VMEM((sections, 2, size), f32),
             pltpu.VMEM((sections, size // 2 + 8, size), f32),
-            pltpu.VMEM((sections, 4, piece, size), f32),
+            pltpu.VMEM((4, sections, piece, size), f32),
             pltpu.VMEM((sections, piece, size), f32),
             pltpu.VMEM((sections, size // 2 + 8, size), f32),
-            pltpu.VMEM((sections, 4, piece, size), f32),
+            pltpu.VMEM((4, sections, piece, size), f32),
             pltpu.VMEM((heads, piece, size), f32),
             pltpu.VMEM((3, 1, size), f32),
             pltpu.VMEM((4 * tps, 1, size), f32),
@@ -568,10 +587,10 @@
             dma((sections,)),
             dma((sections,)),
             dma((sections,)),
-            dma((sections, 3)),
+            dma((sections // 2, 3)),
             dma((sections,)),
             dma((sections,)),
-            dma((sections, 3)),
+            dma((sections // 2, 3)),
             dma((heads,)),
             dma((4 * tps,)),
             dma((4 * tps,)),

time: 59.5 us -> 58.9 us (0.990)
  no operation moved by 1% of the time
where the time goes in v6:
time: 58.9 us; the launch traced here: 58.7 us
  Pallas kernels  55 us (93%)
  local copies, waits for them, and re-layouts  3.06 us (5%)
  between operations  0.64 us (1%)
    pallas_call x1, Pallas kernels, shards(): pl.pallas_call(functools.partial(relay_kernel, loss_scale, float(param_co...  55 us
    broadcast_in_dim x1, local copies, waits for them, and re-layouts, shards(): grads[None, :, :size // 8]  1.55 us
    another operation x1, local copies, waits for them, and re-layouts, shards(): grads[:, size // 8 + 1].reshape(1, features)  1.5 us

profile of v6, /device:TPU:1, one launch (start us, length us, event | category | flops | bytes accessed | tf_op | source)
XLA Modules:
  0.0 58.7 jit_solution(15113096140860450902)
XLA Ops:
  0.6 55.0 %relay.1 = f32[14,24,128]{2,1,0:T(8,128)} custom-call(bf16[4,48,1792]{2,1,0:T(8,128)(2,1)} %x_ref.1, f32[1,1792]{1,0:T(1,128)} %gain_ref.1, f32[1,1792]{1,0:T(1,128)} %bias_ref.1, bf16[14,128,128]{2,1,0:T(8,128)(2,1)} %bitcast.7), custom_call_target="tpu_custom_call" | custom-call | flops 301989888 | bytes 4194304 | tf_op jit(solution)/shard_map/relay/pallas_call | solution.py:548
  55.6 1.5 %slice_bitcast_fusion.1 = (f32[1,1792]{1,0:T(1,128)}, f32[1,1792]{1,0:T(1,128)}) fusion(f32[14,24,128]{2,1,0:T(8,128)} %relay.1), kind=kLoop, calls=%fused_computation.1 | loop fusion | bytes 28672 | tf_op jit(solution)/shard_map/reshape;squeeze | solution.py:610
  57.1 1.6 %slice_bitcast_fusion = f32[1,14,16,128]{3,2,1,0:T(8,128)} fusion(f32[14,24,128]{2,1,0:T(8,128)} %relay.1), kind=kLoop, calls=%fused_computation | loop fusion | bytes 229376 | tf_op jit(solution)/shard_map/broadcast_in_dim | solution.py:611

commit v7 on v6

--- a/solution.py
+++ b/solution.py
@@ -433,6 +433,62 @@
         to_dp = lax.rem(dp + lax.rem(step, dps), dps)
         return to_x * dps + to_dp, dict(section=to_x * 4 + column, dp=to_dp)
 
+    def early_copies_left():
+        for other_pair in range(pairs):
+            item, goes, mine, to_dp, to_tp = x_plan(other_pair)
+
+            @pl.when(goes & jnp.logical_not(mine))
+            def _():
+                columns = pl.ds(pl.multiple_of(item * size, size), size)
+                remote(
+                    x_ref.at[:, :, columns], x_in, x_sent.at[other_pair], x_came, tp=to_tp, dp=to_dp
+                ).wait_send()
+
+        @pl.loop(low, high_end)
+        def _(to_unit):
+            for bit in range(2):
+                to_section = to_unit * 2 + bit
+                for to_core in range(2):
+
+                    @pl.when(jnp.logical_not((to_section == section) & (core == to_core)))
+                    def _():
+                        rows = pl.ds(to_core * half, half)
+                        remote(
+                            stage.at[0],
+                            params.at[section],
+                            p_sent.at[to_section, to_core],
+                            p_came.at[section],
+                            tp=sibling,
+                        ).wait_send()
+                        remote(
+                            mix_ref.at[0, rows],
+                            weights.at[section, rows],
+                            w_sent.at[to_section, to_core],
+                            w_came.at[section],
+                            tp=sibling,
+                        ).wait_send()
+
+        @pl.when(active)
+        def _():
+            @pl.loop(0, layers)
+            def _(layer):
+                forward_half(layer).wait_send()
+
+            @pl.loop(0, layers // 2)
+            def _(couple):
+                exchange1(couple).wait_send()
+                for flip in (1, 2, 3):
+                    exchange2(couple, flip).wait_send()
+
+    def owner_copies_left():
+        @pl.when(active)
+        def _():
+            @pl.loop(0, layers)
+            def _(layer):
+                @pl.when(jnp.logical_not(is_owner(layer)))
+                def _():
+                    to_owner(layer).wait_send()
+
     stages = (
         (column_place, all_column, column_sent, column_came),
         (plane_place, all_plane, plane_sent, plane_came),
@@ -461,6 +517,15 @@
                 def _(layer):
                     start_to_owner(lax.rem(layer + section, layers))
 
+        if index == 0:
+            early_copies_left()
+        else:
+            owner_copies_left()
+
+        @pl.loop(1, count)
+        def _(step):
+            copy_to(step).wait_send()
+
         for step in range(1, count):
             copy_from(step).wait_recv()
         square[index + 1] = jnp.sum(slots[...], axis=0)
@@ -473,65 +538,6 @@
             out4.at[0, 0:long], in4.at[item, 0:long], sent4.at[0], came4.at[item], tp=sibling
         ).wait_recv()
         grads_ref[item, 0:long] = in4[item, 0:long] * scale
-
-    for index, (place_of, slots, sent, came) in enumerate(stages):
-
-        @pl.loop(1, slots.shape[0])
-        def _(step, index=index, place_of=place_of, slots=slots, sent=sent, came=came):
-            place, where = place_of(step)
-            remote(
-                square.at[index], slots.at[place], sent.at[place], came.at[place], **where
-            ).wait_send()
-
-    for other_pair in range(pairs):
-        item, goes, mine, to_dp, to_tp = x_plan(other_pair)
-
-        @pl.when(goes & jnp.logical_not(mine))
-        def _():
-            columns = pl.ds(pl.multiple_of(item * size, size), size)
-            remote(
-                x_ref.at[:, :, columns], x_in, x_sent.at[other_pair], x_came, tp=to_tp, dp=to_dp
-            ).wait_send()
-
-    @pl.loop(low, high_end)
-    def _(to_unit):
-        for bit in range(2):
-            to_section = to_unit * 2 + bit
-            for to_core in range(2):
-
-                @pl.when(jnp.logical_not((to_section == section) & (core == to_core)))
-                def _():
-                    rows = pl.ds(to_core * half, half)
-                    remote(
-                        stage.at[0],
-                        params.at[section],
-                        p_sent.at[to_section, to_core],
-                        p_came.at[section],
-                        tp=sibling,
-                    ).wait_send()
-                    remote(
-                        mix_ref.at[0, rows],
-                        weights.at[section, rows],
-                        w_sent.at[to_section, to_core],
-                        w_came.at[section],
-                        tp=sibling,
-                    ).wait_send()
-
-    @pl.when(active)
-    def _():
-        @pl.loop(0, layers)
-        def _(layer):
-            forward_half(layer).wait_send()
-
-            @pl.when(jnp.logical_not(is_owner(layer)))
-            def _():
-                to_owner(layer).wait_send()
-
-        @pl.loop(0, layers // 2)
-        def _(couple):
-            exchange1(couple).wait_send()
-            for flip in (1, 2, 3):
-                exchange2(couple, flip).wait_send()
 
 
 def shards(inputs, norm_gain, norm_bias, mix):

time: 58.9 us -> 57.9 us (0.983)
  Pallas kernels: 55 us -> 53.9 us
    pallas_call x1, Pallas kernels: 55 us -> 53.9 us  [shards(): pl.pallas_call(functools.partial(relay_kernel, loss_scale, float(param_co...]
where the time goes in v7:
time: 57.9 us; the launch traced here: 57.6 us
  Pallas kernels  53.9 us (93%)
  local copies, waits for them, and re-layouts  3.06 us (5%)
  between operations  0.64 us (1%)
    pallas_call x1, Pallas kernels, shards(): pl.pallas_call(functools.partial(relay_kernel, loss_scale, float(param_co...  53.9 us
    broadcast_in_dim x1, local copies, waits for them, and re-layouts, shards(): grads[None, :, :size // 8]  1.55 us
    another operation x1, local copies, waits for them, and re-layouts, shards(): grads[:, size // 8 + 1].reshape(1, features)  1.5 us

profile of v7, /device:TPU:1, one launch (start us, length us, event | category | flops | bytes accessed | tf_op | source)
XLA Modules:
  0.0 57.6 jit_solution(14493010706233228347)
XLA Ops:
  0.6 53.9 %relay.1 = f32[14,24,128]{2,1,0:T(8,128)} custom-call(bf16[4,48,1792]{2,1,0:T(8,128)(2,1)} %x_ref.1, f32[1,1792]{1,0:T(1,128)} %gain_ref.1, f32[1,1792]{1,0:T(1,128)} %bias_ref.1, bf16[14,128,128]{2,1,0:T(8,128)(2,1)} %bitcast.7), custom_call_target="tpu_custom_call" | custom-call | flops 301989888 | bytes 4194304 | tf_op jit(solution)/shard_map/relay/pallas_call | solution.py:554
  54.5 1.5 %slice_bitcast_fusion.1 = (f32[1,1792]{1,0:T(1,128)}, f32[1,1792]{1,0:T(1,128)}) fusion(f32[14,24,128]{2,1,0:T(8,128)} %relay.1), kind=kLoop, calls=%fused_computation.1 | loop fusion | bytes 28672 | tf_op jit(solution)/shard_map/reshape;squeeze | solution.py:616
  56.1 1.6 %slice_bitcast_fusion = f32[1,14,16,128]{3,2,1,0:T(8,128)} fusion(f32[14,24,128]{2,1,0:T(8,128)} %relay.1), kind=kLoop, calls=%fused_computation | loop fusion | bytes 229376 | tf_op jit(solution)/shard_map/broadcast_in_dim | solution.py:617

commit v8 on v7

--- a/solution.py
+++ b/solution.py
@@ -173,6 +173,11 @@
     greet(tp=high * 2 + 1 - core)
     greeted += 2
     square[...] = jnp.zeros_like(square)
+    for index, ref in enumerate((gain_ref, bias_ref)):
+        pltpu.make_async_copy(ref, rows_in.at[index], rows_came.at[index]).wait()
+        for item in range(heads):
+            columns = slice(item * size, (item + 1) * size)
+            stage[item, index : index + 1] = rows_in[index, 0:1, columns]
     pl.semaphore_wait(barrier, greeted)
 
     def x_plan(other_pair):
@@ -199,11 +204,6 @@
                 dp=to_dp,
             )
 
-    for index, ref in enumerate((gain_ref, bias_ref)):
-        pltpu.make_async_copy(ref, rows_in.at[index], rows_came.at[index]).wait()
-        for item in range(heads):
-            columns = slice(item * size, (item + 1) * size)
-            stage[item, index : index + 1] = rows_in[index, 0:1, columns]
     middle = lax.div(heads + pairs - 1 - pair, pairs)
     stop = lax.div(2 * heads + pairs - 1 - pair, pairs)
     low = jnp.where(core == 0, 0, middle)

time: 57.9 us -> 57.9 us (level)
  no operation moved by 1% of the time
where the time goes in v8:
time: 57.9 us; the launch traced here: 57.6 us
  Pallas kernels  53.9 us (93%)
  local copies, waits for them, and re-layouts  3.06 us (5%)
  between operations  0.64 us (1%)
    pallas_call x1, Pallas kernels, shards(): pl.pallas_call(functools.partial(relay_kernel, loss_scale, float(param_co...  53.9 us
    broadcast_in_dim x1, local copies, waits for them, and re-layouts, shards(): grads[None, :, :size // 8]  1.55 us
    another operation x1, local copies, waits for them, and re-layouts, shards(): grads[:, size // 8 + 1].reshape(1, features)  1.5 us

profile of v8, /device:TPU:1, one launch (start us, length us, event | category | flops | bytes accessed | tf_op | source)
XLA Modules:
  0.0 57.6 jit_solution(11551222142809329785)
XLA Ops:
  0.6 53.9 %relay.1 = f32[14,24,128]{2,1,0:T(8,128)} custom-call(bf16[4,48,1792]{2,1,0:T(8,128)(2,1)} %x_ref.1, f32[1,1792]{1,0:T(1,128)} %gain_ref.1, f32[1,1792]{1,0:T(1,128)} %bias_ref.1, bf16[14,128,128]{2,1,0:T(8,128)(2,1)} %bitcast.7), custom_call_target="tpu_custom_call" | custom-call | flops 301989888 | bytes 4194304 | tf_op jit(solution)/shard_map/relay/pallas_call | solution.py:554
  54.5 1.5 %slice_bitcast_fusion.1 = (f32[1,1792]{1,0:T(1,128)}, f32[1,1792]{1,0:T(1,128)}) fusion(f32[14,24,128]{2,1,0:T(8,128)} %relay.1), kind=kLoop, calls=%fused_computation.1 | loop fusion | bytes 28672 | tf_op jit(solution)/shard_map/reshape;squeeze | solution.py:616
  56.0 1.6 %slice_bitcast_fusion = f32[1,14,16,128]{3,2,1,0:T(8,128)} fusion(f32[14,24,128]{2,1,0:T(8,128)} %relay.1), kind=kLoop, calls=%fused_computation | loop fusion | bytes 229376 | tf_op jit(solution)/shard_map/broadcast_in_dim | solution.py:617

commit v9 on v7

--- a/solution.py
+++ b/solution.py
@@ -416,9 +416,9 @@
         for couple in range(LAG, 0, -1):
             sum_pair(couple)
             to_chips(couple)
-        sum_chips((6, 7))
         sum_pair(0)
         to_chips(0)
+        sum_chips((6, 7))
         sum_chips((4, 5))
         sum_chips((3, 2))
         sum_chips((1, 0))

time: 57.9 us -> 57.9 us (level)
  no operation moved by 1% of the time
where the time goes in v9:
time: 57.9 us; the launch traced here: 57.6 us
  Pallas kernels  53.9 us (93%)
  local copies, waits for them, and re-layouts  3.06 us (5%)
  between operations  0.64 us (1%)
    pallas_call x1, Pallas kernels, shards(): pl.pallas_call(functools.partial(relay_kernel, loss_scale, float(param_co...  53.9 us
    broadcast_in_dim x1, local copies, waits for them, and re-layouts, shards(): grads[None, :, :size // 8]  1.55 us
    another operation x1, local copies, waits for them, and re-layouts, shards(): grads[:, size // 8 + 1].reshape(1, features)  1.5 us

profile of v9, /device:TPU:1, one launch (start us, length us, event | category | flops | bytes accessed | tf_op | source)
XLA Modules:
  0.0 57.6 jit_solution(3031521043773543873)
XLA Ops:
  0.6 53.9 %relay.1 = f32[14,24,128]{2,1,0:T(8,128)} custom-call(bf16[4,48,1792]{2,1,0:T(8,128)(2,1)} %x_ref.1, f32[1,1792]{1,0:T(1,128)} %gain_ref.1, f32[1,1792]{1,0:T(1,128)} %bias_ref.1, bf16[14,128,128]{2,1,0:T(8,128)(2,1)} %bitcast.7), custom_call_target="tpu_custom_call" | custom-call | flops 301989888 | bytes 4194304 | tf_op jit(solution)/shard_map/relay/pallas_call | solution.py:554
  54.5 1.5 %slice_bitcast_fusion.1 = (f32[1,1792]{1,0:T(1,128)}, f32[1,1792]{1,0:T(1,128)}) fusion(f32[14,24,128]{2,1,0:T(8,128)} %relay.1), kind=kLoop, calls=%fused_computation.1 | loop fusion | bytes 28672 | tf_op jit(solution)/shard_map/reshape;squeeze | solution.py:616
  56.1 1.6 %slice_bitcast_fusion = f32[1,14,16,128]{3,2,1,0:T(8,128)} fusion(f32[14,24,128]{2,1,0:T(8,128)} %relay.1), kind=kLoop, calls=%fused_computation | loop fusion | bytes 229376 | tf_op jit(solution)/shard_map/broadcast_in_dim | solution.py:617
